TPU v7x, 512 devices: a whole 4x4x16 slice. The times are simulated.
512 devices in a mesh: pipe: 32 (over x, z_lo), tp: 16 (over y, z_hi, core).
Axes of the slice: x: 4, y: 4, z: 16 (z_hi: 2, z_lo: 8; z = z_hi * 8 + z_lo), core: 2. Of those that a mesh axis runs over, the one named last changes fastest.
Arguments:
- mixed_fwd: bfloat16 [32, 128, 8192], P('pipe', None, 'tp'), may hold values from -6 to 6
- resid_fwd: bfloat16 [32, 128, 4096], P('pipe', 'tp'), may hold values from -6 to 6
- weight_vals: bfloat16 [32, 8192, 4096], P('pipe', 'tp'), as said below
- weight_exps: int32 [32, 256], P('pipe', 'tp'), may hold values from 117 to 121
- inner_x: bfloat16 [32, 128, 8192], P('pipe', None, 'tp'), may hold values from -6 to 6
- inner_z: bfloat16 [32, 128, 8192], P('pipe', None, 'tp'), may hold values from -6 to 6
- proj_b: bfloat16 [32, 128, 2048], P('pipe', None, 'tp'), may hold values from -2 to 2
- proj_c: bfloat16 [32, 128, 2048], P('pipe', None, 'tp'), may hold values from -2 to 2
- step_raw: bfloat16 [32, 128, 128], P('pipe', None, 'tp'), may hold values from -3 to 9
- step_bias: float32 [32, 128], P('pipe', 'tp'), may hold values from -0.5 to 0.5
- decay_log: float32 [32, 128], P('pipe', 'tp'), as said below
- head_skip_weight: float32 [32, 128], P('pipe', 'tp'), may hold values from 0.5 to 1.5
- norm_gain: float32 [32, 8192], P('pipe', 'tp'), may hold values from 0.25 to 1.75
- upstream: bfloat16 [32, 128, 4096], P('pipe', 'tp'), may hold values from -6 to 6
Outputs:
- arriving: bfloat16 [32, 128, 4096], P('pipe', 'tp')
- grad_x: bfloat16 [32, 128, 8192], P('pipe', None, 'tp')
- grad_z: bfloat16 [32, 128, 8192], P('pipe', None, 'tp')
- grad_b: bfloat16 [32, 128, 2048], P('pipe', None, 'tp')
- grad_c: bfloat16 [32, 128, 2048], P('pipe', None, 'tp')
- grad_step: bfloat16 [32, 128, 128], P('pipe', None, 'tp')
- grad_bias: float32 [32, 128], P('pipe', 'tp')
- grad_decay: float32 [32, 128], P('pipe', 'tp')
- grad_skip: float32 [32, 128], P('pipe', 'tp')
- grad_gain: float32 [32, 8192], P('pipe', 'tp')
Inputs may be any that keep to these rules, and one draw needn't show every extreme that they name: `weight_vals`: every entry is plus or minus (1 + m / 8) times 2 ** k with whole m from 0 to 7 and k from -2 to 0. exp(decay_log) * 128 lies between 1 and 13.
All inputs are finite; a program needn't handle non-finite values.
Results may differ from a plain program's by a relative error of at most 0.015.
Values may be sent and summed in bfloat16 or wider, within the bound.
A program may use at most 64 MiB of HBM per device.

v0:
```python
import jax
import jax.numpy as jnp
from jax import lax
from jax.sharding import PartitionSpec as P

BLOCK = 64
SCALE_BLOCK = 32


EPSILON = 1e-05
HIGHEST = lax.Precision.HIGHEST


def shifted(block, axis, distance):
    devices = range(lax.axis_size(axis))
    route = [(i - distance, i) for i in devices if i - distance in devices]
    return lax.ppermute(block, axis, route)


def block_scale(exponents):
    depth_left = 127 - exponents
    factor = jnp.ones(exponents.shape, jnp.float32)
    for position in range(7):
        switched = depth_left // 2**position % 2 == 1
        factor = factor * jnp.where(switched, jnp.float32(0.5**2**position), jnp.float32(1.0))
    return factor


def carry_step(carried, pieces):
    decay_now, state_now = pieces
    return (decay_now[:, None, None] * carried + state_now, carried)


def local_mixer(
    inputs, gate_in, proj_b, proj_c, step_raw, step_bias, decay_log, head_skip_weight, norm_gain
):
    length = inputs.shape[0]
    head_count = step_bias.shape[0]
    blocks = length // BLOCK
    step_size = jax.nn.softplus(step_raw + step_bias[None, :])
    decay_rate = -jnp.exp(decay_log)
    per_step = (step_size * decay_rate[None, :]).reshape(blocks, BLOCK, head_count)
    cumulated = jnp.cumsum(per_step, axis=1)
    per_head = inputs.reshape(blocks, BLOCK, head_count, -1)
    weighted = per_head * step_size.reshape(blocks, BLOCK, head_count)[..., None]
    keys_b = proj_b.reshape(blocks, BLOCK, -1)
    query_c = proj_c.reshape(blocks, BLOCK, -1)
    intersection = jnp.einsum(
        "nqs,nks->nqk",
        query_c.astype(jnp.bfloat16),
        keys_b.astype(jnp.bfloat16),
        preferred_element_type=jnp.float32,
    )
    spread_log = cumulated[:, :, None, :] - cumulated[:, None, :, :]
    causal = jnp.tril(jnp.ones((BLOCK, BLOCK), dtype=bool))[None, :, :, None]
    decay_table = jnp.where(causal, jnp.exp(jnp.where(causal, spread_log, 0.0)), 0.0)
    within = jnp.einsum(
        "nqkh,nqk,nkhp->nqhp", decay_table, intersection, weighted, precision=HIGHEST
    )
    decay_to_end = jnp.exp(cumulated[:, -1:, :] - cumulated)
    states = jnp.einsum("nkh,nkhp,nks->nhps", decay_to_end, weighted, keys_b, precision=HIGHEST)
    block_decay = jnp.exp(cumulated[:, -1, :])
    initial = jnp.zeros(states.shape[1:], jnp.float32)
    _, entering = lax.scan(carry_step, initial, (block_decay, states))
    across = (
        jnp.einsum("nqs,nhps->nqhp", query_c, entering, precision=HIGHEST)
        * jnp.exp(cumulated)[..., None]
    )
    result = within + across + head_skip_weight[None, None, :, None] * per_head
    gated_out = result.reshape(length, -1) * jax.nn.silu(gate_in)
    norm_scale = lax.rsqrt(jnp.mean(gated_out * gated_out, axis=-1, keepdims=True) + EPSILON)
    return gated_out * norm_scale * norm_gain[None, :]


def on_device(
    mixed_fwd,
    resid_fwd,
    weight_vals,
    weight_exps,
    inner_x,
    inner_z,
    proj_b,
    proj_c,
    step_raw,
    step_bias,
    decay_log,
    head_skip_weight,
    norm_gain,
    upstream,
):
    channel_scale = jnp.repeat(block_scale(weight_exps[0]), SCALE_BLOCK)
    weight_codes = weight_vals[0]
    scaled = mixed_fwd[0] * channel_scale.astype(jnp.bfloat16)[None, :]
    summed = lax.psum_scatter(
        jnp.dot(scaled, weight_codes, preferred_element_type=jnp.float32).astype(jnp.bfloat16),
        "tp",
        scatter_dimension=0,
        tiled=True,
    ).astype(jnp.float32)
    produced = (resid_fwd[0].astype(jnp.float32) + summed).astype(jnp.bfloat16)
    arriving = shifted(produced, "pipe", 1)
    received = shifted(upstream[0], "pipe", -1)
    cotangent = lax.dot_general(
        lax.all_gather(received, "tp", axis=0, tiled=True),
        weight_codes,
        (((1,), (1,)), ((), ())),
        preferred_element_type=jnp.float32,
    )
    cotangent = cotangent * channel_scale[None, :]
    primals = (
        inner_x[0].astype(jnp.float32),
        inner_z[0].astype(jnp.float32),
        proj_b[0].astype(jnp.float32),
        proj_c[0].astype(jnp.float32),
        step_raw[0].astype(jnp.float32),
        step_bias[0],
        decay_log[0],
        head_skip_weight[0],
        norm_gain[0],
    )
    _, pullback = jax.vjp(local_mixer, *primals)
    gradients = pullback(cotangent)
    return (
        arriving[None],
        gradients[0].astype(jnp.bfloat16)[None],
        gradients[1].astype(jnp.bfloat16)[None],
        gradients[2].astype(jnp.bfloat16)[None],
        gradients[3].astype(jnp.bfloat16)[None],
        gradients[4].astype(jnp.bfloat16)[None],
        gradients[5][None],
        gradients[6][None],
        gradients[7][None],
        gradients[8][None],
    )


def solution(mesh):
    in_specs = (
        P("pipe", None, "tp"),
        P("pipe", "tp", None),
        P("pipe", "tp", None),
        P("pipe", "tp"),
        P("pipe", None, "tp"),
        P("pipe", None, "tp"),
        P("pipe", None, "tp"),
        P("pipe", None, "tp"),
        P("pipe", None, "tp"),
        P("pipe", "tp"),
        P("pipe", "tp"),
        P("pipe", "tp"),
        P("pipe", "tp"),
        P("pipe", "tp", None),
    )
    out_specs = (
        P("pipe", "tp", None),
        P("pipe", None, "tp"),
        P("pipe", None, "tp"),
        P("pipe", None, "tp"),
        P("pipe", None, "tp"),
        P("pipe", None, "tp"),
        P("pipe", "tp"),
        P("pipe", "tp"),
        P("pipe", "tp"),
        P("pipe", "tp"),
    )
    return jax.shard_map(
        on_device, mesh=mesh, in_specs=in_specs, out_specs=out_specs, check_vma=False
    )
```

profile of v0, /device:TPU:1, one launch (start us, length us, event | category | flops | bytes accessed | tf_op | source)
XLA Modules:
  0.0 243.0 jit_solution(12604491341647695017)
XLA Ops:
  7.3 1.4 collective-permute-start.1
  8.7 0.7 fusion.77
  9.5 0.1 reshape.315
  9.6 4.0 %convolution_convert_fusion = bf16[128,4096]{1,0:T(8,128)(2,1)} fusion(bf16[1,512,4096]{2,1,0:T(8,128)(2,1)} %param.20, bf16[1,128,512]{2,1,0:T(8,128)(2,1)} %param.18, bf16[512]{0:T(512)(128)(2,1)S(1)} %convert_element_type.133), kind=kOutput, calls=%fused_computation.11 | convolution fusion | flops 537460736 | bytes 5374976 | tf_op jit(solution)/shard_map/dot_general | solution.py:95
  13.7 0.1 reshape.324
  13.8 0.1 broadcast_multiply_fusion
  13.8 0.3 copy-done.23
  14.2 0.1 copy.194
  14.3 0.1 reduce_window_sum.22
  14.5 0.5 copy-done.2
  15.0 0.1 reshape.325
  15.2 0.2 copy.197
  15.4 0.4 fusion.29
  15.9 0.4 while.34
  16.0 0.1 bitcast_add_fusion.3
  16.2 0.1 bitcast_add_fusion.3
  16.4 0.1 reshape.326
  16.6 0.2 copy.202
  16.8 0.6 copy-done.14
  17.5 0.1 fusion.91
  17.7 0.4 convolution_bitcast_fusion.1
  18.1 0.8 copy-done.1
  18.9 1.3 multiply_reduce_fusion.4
  20.1 109.4 %reduce-scatter.2.cloned.1.call-done = bf16[8,4096]{1,0:T(8,128)(2,1)} async-done(((bf16[128,4096]{1,0:T(8,128)(2,1)}), bf16[8,4096]{1,0:T(8,128)(2,1)}) %reduce-scatter.2.cloned.1.call-update) | async-done | bytes 65552 | tf_op jit(solution)/shard_map/reduce_scatter | solution.py:94
  129.5 0.9 fusion.62
  130.4 1.5 collective-permute-start
  131.9 0.1 add.159
  132.0 0.2 copy.203
  132.2 0.1 reshape.316
  132.4 0.6 collective-permute-done
  133.0 71.3 %all-gather.2.cloned.1.call-done = bf16[128,4096]{1,0:T(8,128)(2,1)} async-done(((bf16[8,4096]{1,0:T(8,128)(2,1)}), bf16[128,4096]{1,0:T(8,128)(2,1)}) %all-gather.2.cloned.1.call-update) | async-done | bytes 1048592 | tf_op jit(solution)/shard_map/all_gather | solution.py:104
  204.3 4.7 %multiply_reduce_fusion.5 = (f32[512]{0:T(512)}, f32[128]{0:T(128)S(1)}, f32[128,512]{1,0:T(8,128)S(1)}) fusion(f32[128]{0:T(128)S(1)} %rsqrt.10, f32[128,512]{1,0:T(8,128)S(1)} %reshape.316, bf16[1,128,512]{2,1,0:T(8,128)(2,1)S(1)} %copy-done.6, f32[512]{0:T(512)S(1)} %bitcast.215, f32[512]{0:T(512)S(1)} %reshape.315, ...), kind=kOutput, calls=%fused_computation.72 | convolution fusion | flops 537722240 | bytes 5905408 | tf_op jit(solution)/shard_map/dot_general | solution.py:103
  209.0 1.5 fusion.40
  210.5 0.1 reshape.317
  210.6 0.2 copy.204
  210.9 1.6 fusion.36
  212.5 0.7 fusion.16
  213.2 0.8 fusion.17
  214.0 1.1 fusion.26
  215.2 0.6 broadcast.255
  215.7 5.2 %while.35 = (s32[]{:T(128)}, f32[8,64,128]{2,1,0:T(8,128)S(1)}, f32[2,8]{1,0:T(2,128)}, f32[2,8,64,128]{3,2,1,0:T(8,128)S(1)}, f32[2,8,64,128]{3,2,1,0:T(8,128)S...) while((s32[]{:T(128)}, f32[8,64,128]{2,1,0:T(8,128)S(1)}, ...), condition=%wide.region_8.9_spmd.clone, body=%wide.region_6.8_spmd.clone.sunk | while | flops 393212 | bytes 1573188 | solution.py:64
  215.8 0.6 fusion.111
  216.4 0.7 fusion.112
  217.0 1.3 dynamic_update_slice.41
  218.3 0.7 fusion.111
  219.0 0.7 fusion.112
  219.7 1.3 dynamic_update_slice.41
  221.0 0.4 convolution_bitcast_fusion
  221.4 2.5 %multiply_reduce_fusion = (f32[2,64,8]{1,2,0:T(8,128)S(1)}, f32[2,64,8]{1,2,0:T(8,128)S(1)}, bf16[2,64,8,64]{1,3,2,0:T(8,128)(2,1)S(1)}, f32[2,64,8]{1,2,0:T(8,128)S(1)}) fusion(f32[2,64,8,64]{1,3,2,0:T(8,128)S(1)} %convolution_bitcast_fusion, f32[2,64,8,64]{1,3,2,0:T(8,128)S(1)} %copy.197, f32[2,64,8]{1,2,0:T(8,128)S(1)} %get-tuple-element.272, ...), kind=kOutput, calls=%fused_computation.36 | convolution fusion | flops 51442688 | bytes 1503264 | tf_op jit(solution)/shard_map/transpose(jvp(nqkh,nqk,nkhp->nqhp))/dot_general | solution.py:57
  223.8 0.1 copy.240
  224.0 0.1 copy.216
  224.1 0.1 copy.219
  224.2 0.1 copy.220
  224.4 0.6 reduce_window_sum.23
  225.0 0.1 reshape.318
  225.1 2.0 fusion.88
  227.1 1.2 bitcast_multiply_fusion.4
  228.3 2.3 fusion.14
  230.6 1.6 fusion.15
  232.2 0.2 copy.208
  232.4 0.9 convert_element_type.146
  233.3 0.8 reduce_sum.148
  234.1 0.6 reduce_sum.149
  234.7 1.5 copy.289
  (88 shorter events, 0.9 us)
Async XLA Ops:
  7.2 10.3 %copy-start = (bf16[1,128,128]{2,1,0:T(8,128)(2,1)S(1)}, bf16[1,128,128]{2,1,0:T(8,128)(2,1)}, u32[]{:S(2)}) copy-start(bf16[1,128,128]{2,1,0:T(8,128)(2,1)} %param.25) | copy-start | bytes 98308
  7.2 6.4 %copy-start.26 = (f32[1,8]{1,0:T(1,128)S(1)}, f32[1,8]{1,0:T(1,128)}, u32[]{:S(2)}) copy-start(f32[1,8]{1,0:T(1,128)} %param.28) | copy-start | bytes 100
  7.2 6.4 %copy-start.20 = (bf16[1,128,8]{1,2,0:T(8,128)(2,1)S(1)}, bf16[1,128,8]{1,2,0:T(8,128)(2,1)}, u32[]{:S(2)}) copy-start(bf16[1,128,8]{1,2,0:T(8,128)(2,1)} %param.26) | copy-start | bytes 6148
  7.2 6.5 %copy-start.22 = (f32[1,8]{1,0:T(1,128)S(1)}, f32[1,8]{1,0:T(1,128)}, u32[]{:S(2)}) copy-start(f32[1,8]{1,0:T(1,128)} %param.27) | copy-start | bytes 100
  7.2 7.8 %copy-start.5 = (bf16[1,128,512]{2,1,0:T(8,128)(2,1)S(1)}, bf16[1,128,512]{2,1,0:T(8,128)(2,1)}, u32[]{:S(2)}) copy-start(bf16[1,128,512]{2,1,0:T(8,128)(2,1)} %param.22) | copy-start | bytes 393220
  7.2 122.3 %reduce-scatter.2.cloned.1.call-start = ((), (), s32[]{:S(2)}) async-start(), calls=%async_computation.1 | async-start | bytes 1114112 | tf_op jit(solution)/shard_map/reduce_scatter | solution.py:94
  7.3 9.5 %collective-permute-start.1 = (bf16[8,4096]{1,0:T(8,128)(2,1)}, bf16[8,4096]{1,0:T(8,128)(2,1)S(1)}, u32[]{:S(2)}, u32[]{:S(2)}) collective-permute-start(bf16[8,4096]{1,0:T(8,128)(2,1)} %bitcast.223), channel_id=1, source_target_pairs={{16,0},{32,16},{48,32},{64,48},{80,64},{96,80},{112,96},{128,112},... | collective-permute-start | bytes 196616 | tf_op jit(solution)/shard_map/ppermute | solution.py:17
  9.6 5.8 %copy-start.4 = (bf16[1,128,128]{2,1,0:T(8,128)(2,1)S(1)}, bf16[1,128,128]{2,1,0:T(8,128)(2,1)}, u32[]{:S(2)}) copy-start(bf16[1,128,128]{2,1,0:T(8,128)(2,1)} %param.24) | copy-start | bytes 98308
  13.6 190.7 %all-gather.2.cloned.1.call-start = ((), (), s32[]{:S(2)}) async-start(), calls=%async_computation.2 | async-start | bytes 1114112 | tf_op jit(solution)/shard_map/all_gather | solution.py:104
  13.7 0.5 copy-start.23
  14.4 1.5 copy-start.16
  14.4 0.6 copy-start.2
  15.4 1.0 copy-start.6
  15.9 3.0 %copy-start.25 = (f32[1,8]{1,0:T(1,128)S(1)}, f32[1,8]{1,0:T(1,128)}, u32[]{:S(2)}) copy-start(f32[1,8]{1,0:T(1,128)} %param.29) | copy-start | bytes 100
  16.3 1.8 copy-start.27
  16.3 113.2 %copy-start.12 = (bf16[1,8,4096]{2,1,0:T(8,128)(2,1)S(1)}, bf16[1,8,4096]{2,1,0:T(8,128)(2,1)}, u32[]{:S(2)}) copy-start(bf16[1,8,4096]{2,1,0:T(8,128)(2,1)} %param.19) | copy-start | bytes 196612
  16.4 194.5 %copy-start.11 = (f32[2,64,8]{1,2,0:T(8,128)}, f32[2,64,8]{1,2,0:T(8,128)S(1)}, u32[]{:S(2)}) copy-start(f32[2,64,8]{1,2,0:T(8,128)S(1)} %copy.195) | copy-start | bytes 12292
  16.4 194.2 %copy-start.10 = (f32[2,64,8]{1,2,0:T(8,128)}, f32[2,64,8]{1,2,0:T(8,128)S(1)}, u32[]{:S(2)}) copy-start(f32[2,64,8]{1,2,0:T(8,128)S(1)} %copy.199) | copy-start | bytes 12292
  16.6 187.7 %copy-start.21 = (f32[1,512]{1,0:T(1,128)S(1)}, f32[1,512]{1,0:T(1,128)}, u32[]{:S(2)}) copy-start(f32[1,512]{1,0:T(1,128)} %param.30) | copy-start | bytes 6148
  16.8 0.6 copy-start.14
  17.5 193.4 %copy-start.15 = (pred[64,64]{1,0:T(8,128)(4,1)}, pred[64,64]{1,0:T(8,128)(4,1)S(1)}, u32[]{:S(2)}) copy-start(pred[64,64]{1,0:T(8,128)(4,1)S(1)} %iota_compare_fusion) | copy-start | bytes 12292
  17.7 195.6 %copy-start.7 = (f32[2,64,64]{2,1,0:T(8,128)}, f32[2,64,64]{2,1,0:T(8,128)S(1)}, u32[]{:S(2)}) copy-start(f32[2,64,64]{2,1,0:T(8,128)S(1)} %fusion.91) | copy-start | bytes 98308
  18.1 0.8 copy-start.1
  130.4 2.6 %collective-permute-start = (bf16[8,4096]{1,0:T(8,128)(2,1)S(1)}, bf16[8,4096]{1,0:T(8,128)(2,1)S(1)}, u32[]{:S(2)}, u32[]{:S(2)}) collective-permute-start(bf16[8,4096]{1,0:T(8,128)(2,1)S(1)} %fusion.62), channel_id=1, source_target_pairs={{0,16},{16,32},{32,48},{48,64},{64,80},{80,96},{96,112},{112,128},... | collective-permute-start | bytes 196616 | tf_op jit(solution)/shard_map/ppermute | solution.py:17
  133.0 71.3 %copy-start.13 = (bf16[8,4096]{1,0:T(8,128)(2,1)}, bf16[8,4096]{1,0:T(8,128)(2,1)S(1)}, u32[]{:S(2)}) copy-start(bf16[8,4096]{1,0:T(8,128)(2,1)S(1)} %collective-permute-done) | copy-start | bytes 196612
  220.9 3.0 %copy-start.3 = (f32[2,64,8]{2,1,0:T(8,128)S(1)}, f32[2,64,8]{2,1,0:T(8,128)}, u32[]{:S(2)}) copy-start(f32[2,64,8]{2,1,0:T(8,128)} %copy-done.2) | copy-start | bytes 12292
  220.9 3.1 %copy-start.17 = (f32[2,1,8]{2,1,0:T(1,128)S(1)}, f32[2,1,8]{2,1,0:T(1,128)}, u32[]{:S(2)}) copy-start(f32[2,1,8]{2,1,0:T(1,128)} %copy-done.16) | copy-start | bytes 196
  220.9 3.1 %copy-start.24 = (f32[2,8]{1,0:T(2,128)S(1)}, f32[2,8]{1,0:T(2,128)}, u32[]{:S(2)}) copy-start(f32[2,8]{1,0:T(2,128)} %get-tuple-element.188) | copy-start | bytes 196
  220.9 3.2 %copy-start.19 = (f32[2,64,8]{1,2,0:T(8,128)S(1)}, f32[2,64,8]{1,2,0:T(8,128)}, u32[]{:S(2)}) copy-start(f32[2,64,8]{1,2,0:T(8,128)} %get-tuple-element.236) | copy-start | bytes 12292
  220.9 3.3 %copy-start.18 = (f32[2,64,8]{1,2,0:T(8,128)S(1)}, f32[2,64,8]{1,2,0:T(8,128)}, u32[]{:S(2)}) copy-start(f32[2,64,8]{1,2,0:T(8,128)} %get-tuple-element.237) | copy-start | bytes 12292
  221.0 7.3 %copy-start.9 = (f32[2,64,128]{2,1,0:T(8,128)S(1)}, f32[2,64,128]{2,1,0:T(8,128)}, u32[]{:S(2)}) copy-start(f32[2,64,128]{2,1,0:T(8,128)} %fusion.16) | copy-start | bytes 196612
  221.0 9.6 %copy-start.8 = (f32[2,64,128]{2,1,0:T(8,128)S(1)}, f32[2,64,128]{2,1,0:T(8,128)}, u32[]{:S(2)}) copy-start(f32[2,64,128]{2,1,0:T(8,128)} %fusion.17) | copy-start | bytes 196612
Sparse Core Ops, SparseCore 0:
  13.7 115.7 reduce-scatter.1
  133.9 70.3 all-gather.1
where the time goes:
time: 243 us
  waiting for transfers between devices  181 us (74%)
  matrix products  21.9 us (9%)
  between operations  14.6 us (6%)
  local copies, waits for them, and re-layouts  12.7 us (5%)
  other arithmetic  9.36 us (4%)
  starting transfers between devices  2.98 us (1%)
    reduce_scatter x1, waiting for transfers between devices, on_device(): lax.psum_scatter(jnp.dot(scaled, weight_codes, preferred_element_type=jnp...  109 us
    all_gather x1, waiting for transfers between devices, on_device(): lax.all_gather(received, 'tp', axis=0, tiled=True)  71.3 us
    dot_general x3, matrix products, local_mixer(): jnp.einsum('nqkh,nqk,nkhp->nqhp', decay_table, intersection, weighted, pr...  5.32 us
  transfers between devices with their start and end apart: 4, of which 3 were waited for; matrix products, arithmetic and copies ran while one was open for 4% of the time, Pallas kernels for 0%

commit v1 on v0

v1 whole, which is shorter than its diff:
```python
import jax
import jax.numpy as jnp
from jax import lax
from jax.experimental import pallas as pl
from jax.experimental.pallas import tpu as pltpu
from jax.sharding import PartitionSpec as P

MESH = pl.DeviceIdType.MESH
HIGHEST = lax.Precision.HIGHEST
F32 = jnp.float32
BF16 = jnp.bfloat16

TOKENS = 128
D = 4096
HALF = D // 2
CHANNELS = 512
HEADS = 8
HEAD_DIM = 64
STATE = 128
ROWS = 8
SCALE_BLOCK = 32
Z_RUN = 8
EPSILON = 1e-05
PARTS = 2
WIDTH = HALF // PARTS


def nt(a, b, precision=None):
    return lax.dot_general(
        a, b, (((1,), (1,)), ((), ())), preferred_element_type=F32, precision=precision
    )


def nn(a, b, precision=None):
    return jnp.dot(a, b, preferred_element_type=F32, precision=precision)


def fold(v):
    n = v.shape[1] // 2
    return jnp.concatenate([v[:, :n], v[:, n:]], axis=0)


def block_scale(exponents):
    depth_left = 127 - exponents
    factor = jnp.ones(exponents.shape, F32)
    for position in range(7):
        switched = ((depth_left >> position) & 1) == 1
        factor = factor * jnp.where(switched, F32(0.5 ** 2**position), F32(1.0))
    return factor


def iota(shape, dim):
    return lax.broadcasted_iota(jnp.int32, shape, dim)


def kernel(
    mixed_hbm, resid_hbm, weight_hbm, exps_hbm, x_hbm, z_hbm, b_hbm, c_hbm, raw_hbm,
    bias_hbm, decay_hbm, skip_hbm, gain_hbm, up_hbm,
    arriving_out, gx_out, gz_out, gb_out, gc_out, gstep_out, gbias_out, gdecay_out, gskip_out, ggain_out,
    mixed, resid, weight, exps, x, z, b, c_in, raw, bias, decay, skip, gain, up,
    up_send, gathered, rows_in, scaled, temp, p_send, p_own, s_recv, q_send, y_recv, r_sum, z_send, z_recv, n_send, n_recv,
    pads, ed, w_t, x_stack, g_table, y_val, normed, q_gate, s_gate,
    arriving, gx, gz, gb, gc, gstep, gbias, gdecay, gskip, ggain,
    load_sem, w_sem, out_sem, ag_send, ag_recv, sib_send, sib_recv, ys_send, ys_recv, zs_send, zs_recv, ns_send, ns_recv,
):
    p, t = lax.axis_index("pipe"), lax.axis_index("tp")
    n_pipe = lax.axis_size("pipe")
    z_lo = p % Z_RUN
    y, z_hi, core = t // 4, (t // 2) % 2, t % 2
    after, before = (p + 1) % n_pipe, (p + n_pipe - 1) % n_pipe
    turn_up = jnp.where(z_lo == Z_RUN - 1, 1, 0)
    turn_down = jnp.where(z_lo == 0, 1, 0)
    near = (z_hi + turn_up) % 2
    near_down = (z_hi + turn_down) % 2
    late = z_hi == 1

    def at(yy, zz, cc):
        return yy * 4 + zz * 2 + cc

    sibling = (p, at(y, z_hi, 1 - core))
    y_peer = [(p, at((y + d) % 4, z_hi, core)) for d in range(4)]
    opposite = (p, at(y, 1 - z_hi, core))

    def load(i, src, dst):
        return pltpu.make_async_copy(src, dst, load_sem.at[i])

    loads = {
        name: load(i, src.at[0] if len(src.shape) == 3 else src, dst)
        for i, (name, src, dst) in enumerate(
            (
                ("up", up_hbm, up), ("mixed", mixed_hbm, mixed), ("exps", exps_hbm, exps), ("resid", resid_hbm, resid),
                ("raw", raw_hbm, raw), ("bias", bias_hbm, bias), ("decay", decay_hbm, decay),
                ("b", b_hbm, b), ("c", c_hbm, c_in), ("x", x_hbm, x), ("z", z_hbm, z),
                ("skip", skip_hbm, skip), ("gain", gain_hbm, gain),
            )
        )
    }

    def columns(side, k):
        half = 1 - core if side == 0 else core
        return pl.ds(pl.multiple_of(half * HALF + k * WIDTH, WIDTH), WIDTH)

    def w_load(side, k):
        cols = columns(side, k)
        return pltpu.make_async_copy(weight_hbm.at[0, :, cols], weight.at[:, cols], w_sem.at[side, k])

    for name in ("up", "mixed", "exps", "resid"):
        loads[name].start()
    for k in range(PARTS):
        for side in range(2):
            w_load(side, k).start()
    for name in ("raw", "bias", "decay", "b", "c", "x", "z", "skip", "gain"):
        loads[name].start()

    far_down = 1 - near_down
    partners = [sibling, *y_peer[1:], opposite]
    partners += [(after, at(y, near, core)), (after, at(y, near, 1 - core)), (after, at(y, 1 - near, core))]
    partners += [(before, at(y, near_down, core)), (before, at(y, near_down, 1 - core)), (before, at(y, far_down, core))]
    barrier = pltpu.get_barrier_semaphore()
    for device in partners:
        pl.semaphore_signal(barrier, inc=1, device_id=device, device_id_type=MESH)

    def remote(src, dst, send, recv, device):
        return pltpu.make_async_remote_copy(
            src_ref=src, dst_ref=dst, send_sem=send, recv_sem=recv, device_id=device, device_id_type=MESH
        )

    loads["up"].wait()
    up_send[...] = fold(up[...].astype(F32)).astype(BF16)

    def gather_copy(i):
        device = (before, at(y, near_down if i == 0 else far_down, core))
        return remote(up_send, gathered.at[t], ag_send.at[i], ag_recv.at[t], device)

    def enter():
        pl.semaphore_wait(barrier, len(partners))
        gather_copy(1).start()
        gather_copy(0).start()

    pl.when(late)(enter)

    def slot(i, d, cc):
        return at((y + d) % 4, near if i == 0 else 1 - near, cc)

    def block_copy(i, d, device, send):
        s = slot(i, d, core)
        return remote(gathered.at[s], gathered.at[s], send, ag_recv.at[s], device)

    def y_gather(i, d):
        return block_copy(i, 0, y_peer[d], ag_send.at[2 + i * 3 + d - 1])

    def sib_gather(i, d):
        return block_copy(i, d, sibling, ag_send.at[8 + i * 4 + d])

    def arrived(s):
        remote(gathered.at[s], gathered.at[s], ag_send.at[0], ag_recv.at[s], sibling).wait_recv()

    loads["mixed"].wait()
    loads["exps"].wait()
    loads["resid"].wait()
    expand = jnp.where(iota((16, CHANNELS), 1) // SCALE_BLOCK == iota((16, CHANNELS), 0), 1.0, 0.0).astype(BF16)
    scale = nn(jnp.broadcast_to(block_scale(exps[...]), (8, 16)).astype(BF16), expand)[:1]
    scaled[...] = (mixed[...].astype(F32) * scale).astype(BF16)
    mine = pl.ds(pl.multiple_of(t * ROWS, ROWS), ROWS)

    def sib_copy(k):
        return remote(p_send.at[k], s_recv.at[k], sib_send.at[k], sib_recv.at[k], sibling)

    for k in range(PARTS):
        for side in range(2):
            w_load(side, k).wait()
            target = temp if side == 0 else p_own.at[k]
            cols = columns(side, k)
            target[...] = nn(scaled[...], weight[:, cols])
            target[mine, :] += resid[:, cols].astype(F32)
            if side == 0:
                p_send[k] = temp[...].astype(BF16)
                pl.when(late)(lambda k=k: sib_copy(k).start())

    def mixer_forward():
        for name in ("raw", "bias", "decay", "b", "c", "x", "z", "skip", "gain"):
            loads[name].wait()
        pads[...] = jnp.zeros_like(pads)
        pads[0, :, :HEADS] = raw[...].astype(F32) + bias[...]
        pads[2, :, :HEADS] = jnp.broadcast_to(decay[...], (TOKENS, HEADS))
        stepped = pads[0]
        size = jnp.maximum(stepped, 0.0) + jnp.log1p(jnp.exp(-jnp.abs(stepped)))
        rate = -jnp.exp(pads[2])
        pads[1] = size
        pads[2] = rate
        row, col = iota((TOKENS, TOKENS), 0), iota((TOKENS, TOKENS), 1)
        lower = jnp.where(row >= col, 1.0, 0.0)
        cumulated = nn(lower, size * rate, HIGHEST)
        cumulated_t = cumulated.T
        size_t = size.T
        g_table[...] = nt(c_in[...], b[...])
        table = g_table[...]
        lane = iota((TOKENS, 128), 1)
        head_of = jnp.where(iota((8, CHANNELS), 1) // HEAD_DIM == iota((8, CHANNELS), 0), 1.0, 0.0)
        skip_row = nn(jnp.broadcast_to(skip[...], (8, HEADS)), head_of, HIGHEST)[:1]
        for pair in range(HEADS // 2):
            cols = slice(pair * 128, pair * 128 + 128)
            xp = x[:, cols].astype(F32)
            x_stack[pair, :TOKENS] = jnp.where(lane < HEAD_DIM, xp, 0.0).astype(BF16)
            x_stack[pair, TOKENS:] = jnp.where(lane < HEAD_DIM, 0.0, xp).astype(BF16)
            ws = []
            for j in range(2):
                h = pair * 2 + j
                spread = cumulated[:, h : h + 1] - cumulated_t[h : h + 1, :]
                e = jnp.exp(jnp.where(row >= col, spread, -1e30)) * size_t[h : h + 1, :]
                ed[h] = e
                w = e * table
                w_t[pair, :, j * TOKENS : (j + 1) * TOKENS] = w.T.astype(BF16)
                ws.append(w.astype(BF16))
            y_val[:, cols] = nn(jnp.concatenate(ws, axis=1), x_stack[pair]) + skip_row[:, cols] * xp
        zf = z[...].astype(F32)
        sig = 1.0 / (1.0 + jnp.exp(-zf))
        silu = zf * sig
        gated = y_val[...] * silu
        r = lax.rsqrt(jnp.mean(gated * gated, axis=1, keepdims=True) + EPSILON)
        normed[...] = gated * r
        s_gate[...] = silu * r
        q_gate[...] = y_val[...] * (sig + silu * (1.0 - sig)) * r

    @pl.when(z_hi == 0)
    def _():
        mixer_forward()
        enter()
        for k in range(PARTS):
            sib_copy(k).start()

    def y_copy(k, d):
        to = (y + d) % 4
        return remote(
            q_send.at[k, pl.ds(pl.multiple_of(to * 32, 32), 32)], y_recv.at[k, d - 1],
            ys_send.at[k, d - 1], ys_recv.at[k, d - 1], y_peer[d],
        )

    for k in range(PARTS):
        sib_copy(k).wait()
        total = p_own[k] + s_recv[k].astype(F32)
        p_own[k] = total
        q_send[k] = total.astype(BF16)
        for d in (2, 1, 3):
            y_copy(k, d).start()

    pl.when(late)(mixer_forward)

    for i in range(2):
        arrived(slot(i, 0, core))
        for d in (2, 1, 3):
            y_gather(i, d).start()
        sib_gather(i, 0).start()

    def z_copy(k):
        return remote(z_send.at[k], z_recv.at[k], zs_send.at[k], zs_recv.at[k], opposite)

    keep = pl.ds(pl.multiple_of(near * 16, 16), 16)
    give = pl.ds(pl.multiple_of((1 - near) * 16, 16), 16)
    for k in range(PARTS):
        for d in (1, 2, 3):
            y_copy(k, d).wait()
        total = p_own[k, pl.ds(pl.multiple_of(y * 32, 32), 32), :]
        for d in range(3):
            total += y_recv[k, d].astype(F32)
        r_sum[k] = total
        z_send[k] = r_sum[k, give, :].astype(BF16)
        z_copy(k).start()

    for i in range(2):
        for d in (1, 3, 2):
            arrived(slot(i, d, core))
            sib_gather(i, d).start()

    def n_copy(k, cc):
        return remote(
            n_send.at[k, cc], n_recv.at[k, core], ns_send.at[k, cc], ns_recv.at[k, core], (after, at(y, near, cc))
        )

    for k in range(PARTS):
        z_copy(k).wait()
        total = r_sum[k, keep, :] + z_recv[k].astype(F32)
        for cc in range(2):
            n_send[k, cc] = fold(total[cc * ROWS : (cc + 1) * ROWS]).astype(BF16)
            n_copy(k, cc).start()

    for i in range(2):
        for d in range(4):
            arrived(slot(i, d, 1 - core))
    for m in range(8):
        first, second = gathered[2 * m].astype(F32), gathered[2 * m + 1].astype(F32)
        for j in range(2):
            part = jnp.concatenate([first[j * 8 : j * 8 + 8], second[j * 8 : j * 8 + 8]], axis=0)
            rows_in[m * 16 : m * 16 + 16, j * HALF : (j + 1) * HALF] = part.astype(BF16)
    fed = jnp.where(p == n_pipe - 1, 0.0, 1.0)
    cotangent = nt(rows_in[...], weight[...]) * (scale * fed)

    n_val = normed[...]
    cn = cotangent * n_val
    ggain[...] = jnp.sum(cn, axis=0, keepdims=True)
    inner = jnp.mean(cn * gain[...], axis=1, keepdims=True)
    base = cotangent * gain[...] - n_val * inner
    gz[...] = (base * q_gate[...]).astype(BF16)
    dy = base * s_gate[...]
    head_cols = jnp.where(iota((CHANNELS, 128), 0) // HEAD_DIM == iota((CHANNELS, 128), 1), 1.0, 0.0)
    skip_cols = jnp.sum(dy * x[...].astype(F32), axis=0, keepdims=True)
    gskip[...] = nn(jnp.broadcast_to(skip_cols, (8, CHANNELS)), head_cols, HIGHEST)[:1, :HEADS]
    head_of = jnp.where(iota((8, CHANNELS), 1) // HEAD_DIM == iota((8, CHANNELS), 0), 1.0, 0.0)
    skip_row = nn(jnp.broadcast_to(skip[...], (8, HEADS)), head_of, HIGHEST)[:1]
    table = g_table[...]
    lane = iota((TOKENS, 128), 1)
    sub = iota((128, TOKENS), 0)
    d_table = jnp.zeros((TOKENS, TOKENS), F32)
    row_sums = jnp.zeros((TOKENS, 128), F32)
    col_sums = jnp.zeros((128, TOKENS), F32)
    for pair in range(HEADS // 2):
        cols = slice(pair * 128, pair * 128 + 128)
        dyp = dy[:, cols]
        d_w = nt(dyp.astype(BF16), x_stack[pair])
        stack = jnp.concatenate(
            [jnp.where(lane < HEAD_DIM, dyp, 0.0), jnp.where(lane < HEAD_DIM, 0.0, dyp)], axis=0
        ).astype(BF16)
        gx[:, cols] = (nn(w_t[pair], stack) + skip_row[:, cols] * dyp).astype(BF16)
        for j in range(2):
            h = pair * 2 + j
            t_h = d_w[:, j * TOKENS : (j + 1) * TOKENS] * ed[h]
            d_table += t_h
            s_h = t_h * table
            row_sums = jnp.where(lane == h, jnp.sum(s_h, axis=1, keepdims=True), row_sums)
            col_sums = jnp.where(sub == h, jnp.sum(s_h, axis=0, keepdims=True), col_sums)
    gc[...] = nn(d_table.astype(BF16), b[...]).astype(BF16)
    gb[...] = nn(d_table.T.astype(BF16), c_in[...]).astype(BF16)
    direct = col_sums.T
    row, col = iota((TOKENS, TOKENS), 0), iota((TOKENS, TOKENS), 1)
    upper = jnp.where(col >= row, 1.0, 0.0)
    carried = nn(upper, row_sums - direct, HIGHEST)
    size, rate = pads[1], pads[2]
    d_size = direct / size + rate * carried
    d_step = d_size / (1.0 + jnp.exp(-pads[0]))
    gstep[...] = d_step[:, :HEADS].astype(BF16)
    gbias[...] = jnp.sum(d_step, axis=0, keepdims=True)[:, :HEADS]
    gdecay[...] = jnp.sum(size * rate * carried, axis=0, keepdims=True)[:, :HEADS]

    held = jnp.where(p == 0, 0.0, 1.0)
    for k in range(PARTS):
        for cc in range(2):
            remote(
                n_send.at[k, 0], n_recv.at[k, cc], ns_send.at[k, 0], ns_recv.at[k, cc], sibling
            ).wait_recv()
            got = n_recv[k, cc].astype(F32) * held
            start = cc * HALF + k * WIDTH
            arriving[:, start : start + WIDTH // 2] = got[:8].astype(BF16)
            arriving[:, start + WIDTH // 2 : start + WIDTH] = got[8:].astype(BF16)

    stores = [
        pltpu.make_async_copy(src, dst.at[0] if len(dst.shape) == 3 else dst, out_sem.at[i])
        for i, (src, dst) in enumerate(
            (
                (arriving, arriving_out), (gx, gx_out), (gz, gz_out), (gb, gb_out), (gc, gc_out), (gstep, gstep_out),
                (gbias, gbias_out), (gdecay, gdecay_out), (gskip, gskip_out), (ggain, ggain_out),
            )
        )
    ]
    for store in stores:
        store.start()
    for store in stores:
        store.wait()
    for i in range(2):
        gather_copy(i).wait_send()
        for d in (1, 2, 3):
            y_gather(i, d).wait_send()
        for d in range(4):
            sib_gather(i, d).wait_send()
    for k in range(PARTS):
        for cc in range(2):
            n_copy(k, cc).wait_send()


def solution(mesh):
    in_specs = (
        P("pipe", None, "tp"),
        P("pipe", "tp", None),
        P("pipe", "tp", None),
        P("pipe", "tp"),
        P("pipe", None, "tp"),
        P("pipe", None, "tp"),
        P("pipe", None, "tp"),
        P("pipe", None, "tp"),
        P("pipe", None, "tp"),
        P("pipe", "tp"),
        P("pipe", "tp"),
        P("pipe", "tp"),
        P("pipe", "tp"),
        P("pipe", "tp", None),
    )
    out_specs = (
        P("pipe", "tp", None),
        P("pipe", None, "tp"),
        P("pipe", None, "tp"),
        P("pipe", None, "tp"),
        P("pipe", None, "tp"),
        P("pipe", None, "tp"),
        P("pipe", "tp"),
        P("pipe", "tp"),
        P("pipe", "tp"),
        P("pipe", "tp"),
    )
    out_shape = [
        jax.ShapeDtypeStruct(shape, dtype)
        for shape, dtype in (
            ((1, ROWS, D), BF16),
            ((1, TOKENS, CHANNELS), BF16),
            ((1, TOKENS, CHANNELS), BF16),
            ((1, TOKENS, STATE), BF16),
            ((1, TOKENS, STATE), BF16),
            ((1, TOKENS, HEADS), BF16),
            ((1, HEADS), F32),
            ((1, HEADS), F32),
            ((1, HEADS), F32),
            ((1, CHANNELS), F32),
        )
    ]
    vmem = pltpu.VMEM
    dma = pltpu.SemaphoreType.DMA
    scratch = [
        vmem((TOKENS, CHANNELS), BF16), vmem((ROWS, D), BF16), vmem((CHANNELS, D), BF16), vmem((1, 16), jnp.int32),
        vmem((TOKENS, CHANNELS), BF16), vmem((TOKENS, CHANNELS), BF16), vmem((TOKENS, STATE), BF16),
        vmem((TOKENS, STATE), BF16), vmem((TOKENS, HEADS), BF16), vmem((1, HEADS), F32), vmem((1, HEADS), F32),
        vmem((1, HEADS), F32), vmem((1, CHANNELS), F32), vmem((ROWS, D), BF16),
        vmem((16, HALF), BF16), vmem((16, 16, HALF), BF16), vmem((TOKENS, D), BF16), vmem((TOKENS, CHANNELS), BF16),
        vmem((TOKENS, WIDTH), F32), vmem((PARTS, TOKENS, WIDTH), BF16), vmem((PARTS, TOKENS, WIDTH), F32),
        vmem((PARTS, TOKENS, WIDTH), BF16), vmem((PARTS, TOKENS, WIDTH), BF16), vmem((PARTS, 3, 32, WIDTH), BF16),
        vmem((PARTS, 32, WIDTH), F32), vmem((PARTS, 16, WIDTH), BF16), vmem((PARTS, 16, WIDTH), BF16),
        vmem((PARTS, 2, 16, WIDTH // 2), BF16), vmem((PARTS, 2, 16, WIDTH // 2), BF16),
        vmem((3, TOKENS, 128), F32), vmem((HEADS, TOKENS, TOKENS), F32), vmem((HEADS // 2, TOKENS, 2 * TOKENS), BF16),
        vmem((HEADS // 2, 2 * TOKENS, 128), BF16), vmem((TOKENS, TOKENS), F32), vmem((TOKENS, CHANNELS), F32),
        vmem((TOKENS, CHANNELS), F32), vmem((TOKENS, CHANNELS), F32), vmem((TOKENS, CHANNELS), F32),
        vmem((ROWS, D), BF16), vmem((TOKENS, CHANNELS), BF16), vmem((TOKENS, CHANNELS), BF16),
        vmem((TOKENS, STATE), BF16), vmem((TOKENS, STATE), BF16), vmem((TOKENS, HEADS), BF16), vmem((1, HEADS), F32),
        vmem((1, HEADS), F32), vmem((1, HEADS), F32), vmem((1, CHANNELS), F32),
        dma((13,)), dma((2, PARTS)), dma((10,)), dma((16,)), dma((16,)), dma((PARTS,)), dma((PARTS,)),
        dma((PARTS, 3)), dma((PARTS, 3)), dma((PARTS,)), dma((PARTS,)), dma((PARTS, 2)), dma((PARTS, 2)),
    ]
    any_space = pl.BlockSpec(memory_space=pl.ANY)
    call = pl.pallas_call(
        kernel,
        out_shape=out_shape,
        in_specs=[any_space] * 14,
        out_specs=[any_space] * 10,
        scratch_shapes=scratch,
        compiler_params=pltpu.CompilerParams(
            collective_id=0, has_side_effects=True, vmem_limit_bytes=48 * 1024 * 1024
        ),
        cost_estimate=pl.CostEstimate(flops=1_200_000_000, bytes_accessed=6_000_000, transcendentals=500_000),
    )

    def on_device(*blocks):
        return tuple(call(*blocks))

    return jax.shard_map(on_device, mesh=mesh, in_specs=in_specs, out_specs=out_specs, check_vma=False)
```

time: 243 us -> 64.9 us (0.27)
  the two profiles are of different devices: /device:TPU:1 before, /device:TPU:7 now
where the time goes in v1:
time: 64.9 us; the launch traced here: 64.4 us
  Pallas kernels  45.6 us (70%)
  local copies, waits for them, and re-layouts  18.1 us (28%)
  between operations  0.67 us (1%)
    pallas_call x1, Pallas kernels, on_device(): return tuple(call(*blocks))  45.6 us
    unnamed x36, local copies, waits for them, and re-layouts  17.5 us

profile of v1, /device:TPU:7, one launch (start us, length us, event | category | flops | bytes accessed | tf_op | source)
XLA Modules:
  0.0 64.4 jit_solution(14455370096643893297)
XLA Ops:
  0.6 0.8 %copy.24.raw_hbm = bf16[1,128,8]{2,1,0:T(8,128)(2,1)S(1)} copy(bf16[1,128,8]{1,2,0:T(8,128)(2,1)} %param.22) | data formatting | bytes 4096 | tf_op args[8]
  1.4 0.0 copy-start
  1.4 2.2 %copy-done = bf16[1,512,4096]{2,1,0:T(8,128)(2,1)S(1)} copy-done((bf16[1,512,4096]{2,1,0:T(8,128)(2,1)S(1)}, bf16[1,512,4096]{2,1,0:T(8,128)(2,1)}, u32[]{:S(2)}) %copy-start) | copy-done | bytes 4194328
  3.6 0.0 copy-start.1
  3.6 0.9 %copy-done.1 = bf16[1,128,512]{2,1,0:T(8,128)(2,1)S(1)} copy-done((bf16[1,128,512]{2,1,0:T(8,128)(2,1)S(1)}, bf16[1,128,512]{2,1,0:T(8,128)(2,1)}, u32[]{:S(2)}) %copy-start.1) | copy-done | bytes 131096
  4.5 0.0 copy-start.2
  4.5 0.9 %copy-done.2 = bf16[1,128,512]{2,1,0:T(8,128)(2,1)S(1)} copy-done((bf16[1,128,512]{2,1,0:T(8,128)(2,1)S(1)}, bf16[1,128,512]{2,1,0:T(8,128)(2,1)}, u32[]{:S(2)}) %copy-start.2) | copy-done | bytes 131096
  5.4 0.0 copy-start.3
  5.4 0.9 %copy-done.3 = bf16[1,128,512]{2,1,0:T(8,128)(2,1)S(1)} copy-done((bf16[1,128,512]{2,1,0:T(8,128)(2,1)S(1)}, bf16[1,128,512]{2,1,0:T(8,128)(2,1)}, u32[]{:S(2)}) %copy-start.3) | copy-done | bytes 131096
  6.3 0.0 copy-start.4
  6.3 0.8 %copy-done.4 = bf16[1,8,4096]{2,1,0:T(8,128)(2,1)S(1)} copy-done((bf16[1,8,4096]{2,1,0:T(8,128)(2,1)S(1)}, bf16[1,8,4096]{2,1,0:T(8,128)(2,1)}, u32[]{:S(2)}) %copy-start.4) | copy-done | bytes 65560
  7.2 0.0 copy-start.5
  7.2 0.8 %copy-done.5 = bf16[1,8,4096]{2,1,0:T(8,128)(2,1)S(1)} copy-done((bf16[1,8,4096]{2,1,0:T(8,128)(2,1)S(1)}, bf16[1,8,4096]{2,1,0:T(8,128)(2,1)}, u32[]{:S(2)}) %copy-start.5) | copy-done | bytes 65560
  8.0 0.0 copy-start.6
  8.0 0.8 %copy-done.6 = bf16[1,128,128]{2,1,0:T(8,128)(2,1)S(1)} copy-done((bf16[1,128,128]{2,1,0:T(8,128)(2,1)S(1)}, bf16[1,128,128]{2,1,0:T(8,128)(2,1)}, u32[]{:S(2)}) %copy-start.6) | copy-done | bytes 32792
  8.8 0.0 copy-start.7
  8.8 0.8 %copy-done.7 = bf16[1,128,128]{2,1,0:T(8,128)(2,1)S(1)} copy-done((bf16[1,128,128]{2,1,0:T(8,128)(2,1)S(1)}, bf16[1,128,128]{2,1,0:T(8,128)(2,1)}, u32[]{:S(2)}) %copy-start.7) | copy-done | bytes 32792
  9.5 0.0 copy-start.8
  9.5 0.7 %copy-done.8 = f32[1,512]{1,0:T(1,128)S(1)} copy-done((f32[1,512]{1,0:T(1,128)S(1)}, f32[1,512]{1,0:T(1,128)}, u32[]{:S(2)}) %copy-start.8) | copy-done | bytes 2072
  10.2 0.0 copy-start.9
  10.2 0.7 %copy-done.9 = s32[1,16]{1,0:T(1,128)S(1)} copy-done((s32[1,16]{1,0:T(1,128)S(1)}, s32[1,16]{1,0:T(1,128)}, u32[]{:S(2)}) %copy-start.9) | copy-done | bytes 88
  10.9 0.0 copy-start.10
  10.9 0.7 %copy-done.10 = f32[1,8]{1,0:T(1,128)S(1)} copy-done((f32[1,8]{1,0:T(1,128)S(1)}, f32[1,8]{1,0:T(1,128)}, u32[]{:S(2)}) %copy-start.10) | copy-done | bytes 56
  11.5 0.0 copy-start.11
  11.5 0.7 %copy-done.11 = f32[1,8]{1,0:T(1,128)S(1)} copy-done((f32[1,8]{1,0:T(1,128)S(1)}, f32[1,8]{1,0:T(1,128)}, u32[]{:S(2)}) %copy-start.11) | copy-done | bytes 56
  12.2 0.0 copy-start.12
  12.2 0.7 %copy-done.12 = f32[1,8]{1,0:T(1,128)S(1)} copy-done((f32[1,8]{1,0:T(1,128)S(1)}, f32[1,8]{1,0:T(1,128)}, u32[]{:S(2)}) %copy-start.12) | copy-done | bytes 56
  12.8 45.6 %shard_map.213 = (bf16[1,8,4096]{2,1,0:T(8,128)(2,1)S(1)}, bf16[1,128,512]{2,1,0:T(8,128)(2,1)S(1)}, bf16[1,128,512]{2,1,0:T(8,128)(2,1)S(1)}, bf16[1,128,128]{2...) custom-call(bf16[1,128,512]{2,1,0:T(8,128)(2,1)S(1)} %copy-done.1, ...), custom_call_target="tpu_custom_call" | custom-call | flops 1200000000 | bytes 6000000 | tf_op jit(solution)/shard_map/pallas_call | solution.py:458
  58.5 0.7 %copy.25 = bf16[1,128,8]{1,2,0:T(8,128)(2,1)} copy(bf16[1,128,8]{2,1,0:T(8,128)(2,1)S(1)} %get-tuple-element.15) | data formatting | bytes 4096 | tf_op jit(solution)/shard_map/pallas_call | solution.py:458
  59.1 0.6 copy.35
  59.8 0.7 %copy.36 = bf16[1,128,512]{2,1,0:T(8,128)(2,1)} copy(bf16[1,128,512]{2,1,0:T(8,128)(2,1)S(1)} %get-tuple-element.31) | data formatting | bytes 262144
  60.4 0.7 %copy.37 = bf16[1,128,512]{2,1,0:T(8,128)(2,1)} copy(bf16[1,128,512]{2,1,0:T(8,128)(2,1)S(1)} %get-tuple-element.32) | data formatting | bytes 262144
  61.1 0.6 copy.38
  61.7 0.6 copy.39
  62.3 0.5 copy.40
  62.8 0.5 copy.41
  63.3 0.5 copy.42
  63.8 0.6 copy.43
Async XLA Ops:
  1.4 2.2 %copy-start = (bf16[1,512,4096]{2,1,0:T(8,128)(2,1)S(1)}, bf16[1,512,4096]{2,1,0:T(8,128)(2,1)}, u32[]{:S(2)}) copy-start(bf16[1,512,4096]{2,1,0:T(8,128)(2,1)} %weight_hbm.1) | copy-start | bytes 12582916
  3.6 0.9 %copy-start.1 = (bf16[1,128,512]{2,1,0:T(8,128)(2,1)S(1)}, bf16[1,128,512]{2,1,0:T(8,128)(2,1)}, u32[]{:S(2)}) copy-start(bf16[1,128,512]{2,1,0:T(8,128)(2,1)} %mixed_hbm.1) | copy-start | bytes 393220
  4.5 0.9 %copy-start.2 = (bf16[1,128,512]{2,1,0:T(8,128)(2,1)S(1)}, bf16[1,128,512]{2,1,0:T(8,128)(2,1)}, u32[]{:S(2)}) copy-start(bf16[1,128,512]{2,1,0:T(8,128)(2,1)} %x_hbm.1) | copy-start | bytes 393220
  5.4 0.9 %copy-start.3 = (bf16[1,128,512]{2,1,0:T(8,128)(2,1)S(1)}, bf16[1,128,512]{2,1,0:T(8,128)(2,1)}, u32[]{:S(2)}) copy-start(bf16[1,128,512]{2,1,0:T(8,128)(2,1)} %z_hbm.1) | copy-start | bytes 393220
  6.3 0.8 %copy-start.4 = (bf16[1,8,4096]{2,1,0:T(8,128)(2,1)S(1)}, bf16[1,8,4096]{2,1,0:T(8,128)(2,1)}, u32[]{:S(2)}) copy-start(bf16[1,8,4096]{2,1,0:T(8,128)(2,1)} %resid_hbm.1) | copy-start | bytes 196612
  7.2 0.8 %copy-start.5 = (bf16[1,8,4096]{2,1,0:T(8,128)(2,1)S(1)}, bf16[1,8,4096]{2,1,0:T(8,128)(2,1)}, u32[]{:S(2)}) copy-start(bf16[1,8,4096]{2,1,0:T(8,128)(2,1)} %up_hbm.1) | copy-start | bytes 196612
  8.0 0.8 %copy-start.6 = (bf16[1,128,128]{2,1,0:T(8,128)(2,1)S(1)}, bf16[1,128,128]{2,1,0:T(8,128)(2,1)}, u32[]{:S(2)}) copy-start(bf16[1,128,128]{2,1,0:T(8,128)(2,1)} %b_hbm.1) | copy-start | bytes 98308
  8.8 0.8 %copy-start.7 = (bf16[1,128,128]{2,1,0:T(8,128)(2,1)S(1)}, bf16[1,128,128]{2,1,0:T(8,128)(2,1)}, u32[]{:S(2)}) copy-start(bf16[1,128,128]{2,1,0:T(8,128)(2,1)} %c_hbm.1) | copy-start | bytes 98308
  9.5 0.7 %copy-start.8 = (f32[1,512]{1,0:T(1,128)S(1)}, f32[1,512]{1,0:T(1,128)}, u32[]{:S(2)}) copy-start(f32[1,512]{1,0:T(1,128)} %gain_hbm.1) | copy-start | bytes 6148
  10.2 0.7 %copy-start.9 = (s32[1,16]{1,0:T(1,128)S(1)}, s32[1,16]{1,0:T(1,128)}, u32[]{:S(2)}) copy-start(s32[1,16]{1,0:T(1,128)} %exps_hbm.1) | copy-start | bytes 196
  10.9 0.7 %copy-start.10 = (f32[1,8]{1,0:T(1,128)S(1)}, f32[1,8]{1,0:T(1,128)}, u32[]{:S(2)}) copy-start(f32[1,8]{1,0:T(1,128)} %bias_hbm.1) | copy-start | bytes 100
  11.5 0.7 %copy-start.11 = (f32[1,8]{1,0:T(1,128)S(1)}, f32[1,8]{1,0:T(1,128)}, u32[]{:S(2)}) copy-start(f32[1,8]{1,0:T(1,128)} %decay_hbm.1) | copy-start | bytes 100
  12.2 0.7 %copy-start.12 = (f32[1,8]{1,0:T(1,128)S(1)}, f32[1,8]{1,0:T(1,128)}, u32[]{:S(2)}) copy-start(f32[1,8]{1,0:T(1,128)} %skip_hbm.1) | copy-start | bytes 100

commit v2 on v1

--- a/solution.py
+++ b/solution.py
@@ -56,12 +56,11 @@
 def kernel(
     mixed_hbm, resid_hbm, weight_hbm, exps_hbm, x_hbm, z_hbm, b_hbm, c_hbm, raw_hbm,
     bias_hbm, decay_hbm, skip_hbm, gain_hbm, up_hbm,
-    arriving_out, gx_out, gz_out, gb_out, gc_out, gstep_out, gbias_out, gdecay_out, gskip_out, ggain_out,
+    arriving, gx, gz, gb, gc, gstep, gbias, gdecay, gskip, ggain,
     mixed, resid, weight, exps, x, z, b, c_in, raw, bias, decay, skip, gain, up,
     up_send, gathered, rows_in, scaled, temp, p_send, p_own, s_recv, q_send, y_recv, r_sum, z_send, z_recv, n_send, n_recv,
     pads, ed, w_t, x_stack, g_table, y_val, normed, q_gate, s_gate,
-    arriving, gx, gz, gb, gc, gstep, gbias, gdecay, gskip, ggain,
-    load_sem, w_sem, out_sem, ag_send, ag_recv, sib_send, sib_recv, ys_send, ys_recv, zs_send, zs_recv, ns_send, ns_recv,
+    load_sem, w_sem, ready, ag_send, ag_recv, sib_send, sib_recv, ys_send, ys_recv, zs_send, zs_recv, ns_send, ns_recv,
 ):
     p, t = lax.axis_index("pipe"), lax.axis_index("tp")
     n_pipe = lax.axis_size("pipe")
@@ -112,13 +111,40 @@
     for name in ("raw", "bias", "decay", "b", "c", "x", "z", "skip", "gain"):
         loads[name].start()
 
+    def flag(condition):
+        return jnp.where(condition, 1, 0)
+
     far_down = 1 - near_down
-    partners = [sibling, *y_peer[1:], opposite]
-    partners += [(after, at(y, near, core)), (after, at(y, near, 1 - core)), (after, at(y, 1 - near, core))]
-    partners += [(before, at(y, near_down, core)), (before, at(y, near_down, 1 - core)), (before, at(y, far_down, core))]
+    odd = z_lo % 2
+    first = flag(z_hi == 0)
+    at_start = first * turn_down
+    at_half = first * turn_up
+    from_half = (1 - first) * turn_down
+    from_end = (1 - first) * turn_up
+    sends_far = odd + at_start
+    gets_far = (1 - odd) + at_half
+    forwards = odd * (1 - from_end)
+    partners = [(device, 1, 0, 1, 0, 0) for device in (sibling, *y_peer[1:])]
+    partners += [
+        (opposite, 1, first, 1, 1 - first, 1),
+        ((after, at(y, near, core)), 1, at_half, 1, from_end, 0),
+        ((after, at(y, near, 1 - core)), 1, at_half, 0, 0, 0),
+        ((after, at(y, 1 - near, core)), 0, 0, gets_far, near, 1),
+        ((before, at(y, near_down, core)), 1, at_start, 1, from_half, 0),
+        ((before, at(y, near_down, 1 - core)), 0, 0, 1, from_half, 0),
+        ((before, at(y, far_down, core)), sends_far, first, 0, 0, 1),
+    ]
     barrier = pltpu.get_barrier_semaphore()
-    for device in partners:
-        pl.semaphore_signal(barrier, inc=1, device_id=device, device_id_type=MESH)
+
+    def tell(semaphore, device):
+        pl.semaphore_signal(semaphore, inc=1, device_id=device, device_id_type=MESH)
+
+    greeted, readied = 0, [0, 0]
+    for device, to_it, to_held, from_it, from_held, which in partners:
+        greet = from_it * (1 - from_held) + to_it * to_held
+        pl.when(greet > 0)(lambda device=device: tell(barrier, device))
+        greeted += flag(to_it * (1 - to_held) + from_it * from_held > 0)
+        readied[which] += to_it * to_held
 
     def remote(src, dst, send, recv, device):
         return pltpu.make_async_remote_copy(
@@ -133,9 +159,11 @@
         return remote(up_send, gathered.at[t], ag_send.at[i], ag_recv.at[t], device)
 
     def enter():
-        pl.semaphore_wait(barrier, len(partners))
-        gather_copy(1).start()
-        gather_copy(0).start()
+        pl.semaphore_wait(barrier, greeted)
+        pl.when(sends_far * z_hi == 1)(gather_copy(1).start)
+        pl.when(at_start == 0)(gather_copy(0).start)
+        for device, _, _, from_it, from_held, which in partners:
+            pl.when(from_it * from_held == 1)(lambda device=device, which=which: tell(ready.at[which], device))
 
     pl.when(late)(enter)
 
@@ -160,11 +188,15 @@
     loads["resid"].wait()
     expand = jnp.where(iota((16, CHANNELS), 1) // SCALE_BLOCK == iota((16, CHANNELS), 0), 1.0, 0.0).astype(BF16)
     scale = nn(jnp.broadcast_to(block_scale(exps[...]), (8, 16)).astype(BF16), expand)[:1]
-    scaled[...] = (mixed[...].astype(F32) * scale).astype(BF16)
-    mine = pl.ds(pl.multiple_of(t * ROWS, ROWS), ROWS)
-
-    def sib_copy(k):
-        return remote(p_send.at[k], s_recv.at[k], sib_send.at[k], sib_recv.at[k], sibling)
+    for part in range(2):
+        for yy in range(4):
+            rows = pl.ds(pl.multiple_of(yy * 32 + (1 - near if part == 0 else near) * 16, 16), 16)
+            scaled[part * 64 + yy * 16 : part * 64 + yy * 16 + 16] = (mixed[rows].astype(F32) * scale).astype(BF16)
+    mine = pl.ds(pl.multiple_of((1 - turn_up) * 64 + y * 16 + core * ROWS, ROWS), ROWS)
+
+    def sib_copy(part, k):
+        rows = pl.ds(part * 64, 64)
+        return remote(p_send.at[k, rows], s_recv.at[k, rows], sib_send.at[part, k], sib_recv.at[part, k], sibling)
 
     for k in range(PARTS):
         for side in range(2):
@@ -175,13 +207,61 @@
             target[mine, :] += resid[:, cols].astype(F32)
             if side == 0:
                 p_send[k] = temp[...].astype(BF16)
-                pl.when(late)(lambda k=k: sib_copy(k).start())
+                for part in range(2):
+                    pl.when(late)(sib_copy(part, k).start)
+
+    def forward_copy():
+        return block_copy(0, 0, opposite, ag_send.at[16])
+
+    @pl.when(late)
+    def _():
+        arrived(slot(0, 0, core))
+        pl.when(forwards == 1)(forward_copy().start)
+
+    @pl.when(z_hi == 0)
+    def _():
+        enter()
+        for part in range(2):
+            for k in range(PARTS):
+                sib_copy(part, k).start()
+
+    def y_copy(part, k, d):
+        to = (y + d) % 4
+        return remote(
+            q_send.at[k, pl.ds(pl.multiple_of(part * 64 + to * 16, 16), 16)], y_recv.at[part, k, d - 1],
+            ys_send.at[part, k, d - 1], ys_recv.at[part, k, d - 1], y_peer[d],
+        )
+
+    def pair_sum(part):
+        rows = slice(part * 64, part * 64 + 64)
+        for k in range(PARTS):
+            sib_copy(part, k).wait()
+            total = p_own[k, rows] + s_recv[k, rows].astype(F32)
+            p_own[k, rows] = total
+            q_send[k, rows] = total.astype(BF16)
+            for d in (2, 1, 3):
+                y_copy(part, k, d).start()
+
+    def section_sum(part, k):
+        for d in (1, 2, 3):
+            y_copy(part, k, d).wait()
+        total = p_own[k, pl.ds(pl.multiple_of(part * 64 + y * 16, 16), 16), :]
+        for d in range(3):
+            total += y_recv[part, k, d].astype(F32)
+        return total
+
+    def z_copy(k):
+        return remote(z_send.at[k], z_recv.at[k], zs_send.at[k], zs_recv.at[k], opposite)
+
+    pair_sum(0)
 
     def mixer_forward():
         for name in ("raw", "bias", "decay", "b", "c", "x", "z", "skip", "gain"):
             loads[name].wait()
         pads[...] = jnp.zeros_like(pads)
-        pads[0, :, :HEADS] = raw[...].astype(F32) + bias[...]
+        pads[1, :HEADS, :] = raw[...].astype(F32)
+        pads[0] = pads[1].T
+        pads[0, :, :HEADS] += bias[...]
         pads[2, :, :HEADS] = jnp.broadcast_to(decay[...], (TOKENS, HEADS))
         stepped = pads[0]
         size = jnp.maximum(stepped, 0.0) + jnp.log1p(jnp.exp(-jnp.abs(stepped)))
@@ -222,67 +302,60 @@
         s_gate[...] = silu * r
         q_gate[...] = y_val[...] * (sig + silu * (1.0 - sig)) * r
 
-    @pl.when(z_hi == 0)
-    def _():
-        mixer_forward()
-        enter()
-        for k in range(PARTS):
-            sib_copy(k).start()
-
-    def y_copy(k, d):
-        to = (y + d) % 4
-        return remote(
-            q_send.at[k, pl.ds(pl.multiple_of(to * 32, 32), 32)], y_recv.at[k, d - 1],
-            ys_send.at[k, d - 1], ys_recv.at[k, d - 1], y_peer[d],
-        )
+    mixer_forward()
 
     for k in range(PARTS):
-        sib_copy(k).wait()
-        total = p_own[k] + s_recv[k].astype(F32)
-        p_own[k] = total
-        q_send[k] = total.astype(BF16)
-        for d in (2, 1, 3):
-            y_copy(k, d).start()
-
-    pl.when(late)(mixer_forward)
-
-    for i in range(2):
-        arrived(slot(i, 0, core))
+        z_send[k] = section_sum(0, k).astype(BF16)
+        pl.when(late)(z_copy(k).start)
+    pair_sum(1)
+
+    def hand_on(i):
         for d in (2, 1, 3):
             y_gather(i, d).start()
         sib_gather(i, 0).start()
 
-    def z_copy(k):
-        return remote(z_send.at[k], z_recv.at[k], zs_send.at[k], zs_recv.at[k], opposite)
-
-    keep = pl.ds(pl.multiple_of(near * 16, 16), 16)
-    give = pl.ds(pl.multiple_of((1 - near) * 16, 16), 16)
-    for k in range(PARTS):
-        for d in (1, 2, 3):
-            y_copy(k, d).wait()
-        total = p_own[k, pl.ds(pl.multiple_of(y * 32, 32), 32), :]
-        for d in range(3):
-            total += y_recv[k, d].astype(F32)
-        r_sum[k] = total
-        z_send[k] = r_sum[k, give, :].astype(BF16)
-        z_copy(k).start()
-
-    for i in range(2):
+    def hand_over(i):
         for d in (1, 3, 2):
             arrived(slot(i, d, core))
             sib_gather(i, d).start()
 
+    @pl.when(z_hi == 0)
+    def _():
+        pl.when(readied[0] > 0)(lambda: pl.semaphore_wait(ready.at[0], readied[0]))
+        pl.when(at_start == 1)(gather_copy(0).start)
+        arrived(slot(0, 0, core))
+
+    hand_on(0)
+
+    @pl.when(z_hi == 0)
+    def _():
+        pl.semaphore_wait(ready.at[1], readied[1])
+        for k in range(PARTS):
+            z_copy(k).start()
+        pl.when(sends_far == 1)(gather_copy(1).start)
+        pl.when(forwards == 1)(forward_copy().start)
+
+    for k in range(PARTS):
+        r_sum[k] = section_sum(1, k)
+    hand_over(0)
     def n_copy(k, cc):
         return remote(
             n_send.at[k, cc], n_recv.at[k, core], ns_send.at[k, cc], ns_recv.at[k, core], (after, at(y, near, cc))
         )
 
-    for k in range(PARTS):
-        z_copy(k).wait()
-        total = r_sum[k, keep, :] + z_recv[k].astype(F32)
-        for cc in range(2):
-            n_send[k, cc] = fold(total[cc * ROWS : (cc + 1) * ROWS]).astype(BF16)
-            n_copy(k, cc).start()
+    def produce():
+        for k in range(PARTS):
+            z_copy(k).wait()
+            total = r_sum[k] + z_recv[k].astype(F32)
+            for cc in range(2):
+                n_send[k, cc] = fold(total[cc * ROWS : (cc + 1) * ROWS]).astype(BF16)
+                n_copy(k, cc).start()
+
+    pl.when(late)(produce)
+    arrived(slot(1, 0, core))
+    hand_on(1)
+    hand_over(1)
+    pl.when(z_hi == 0)(produce)
 
     for i in range(2):
         for d in range(4):
@@ -300,7 +373,7 @@
     ggain[...] = jnp.sum(cn, axis=0, keepdims=True)
     inner = jnp.mean(cn * gain[...], axis=1, keepdims=True)
     base = cotangent * gain[...] - n_val * inner
-    gz[...] = (base * q_gate[...]).astype(BF16)
+    gz[0] = (base * q_gate[...]).astype(BF16)
     dy = base * s_gate[...]
     head_cols = jnp.where(iota((CHANNELS, 128), 0) // HEAD_DIM == iota((CHANNELS, 128), 1), 1.0, 0.0)
     skip_cols = jnp.sum(dy * x[...].astype(F32), axis=0, keepdims=True)
@@ -320,7 +393,7 @@
         stack = jnp.concatenate(
             [jnp.where(lane < HEAD_DIM, dyp, 0.0), jnp.where(lane < HEAD_DIM, 0.0, dyp)], axis=0
         ).astype(BF16)
-        gx[:, cols] = (nn(w_t[pair], stack) + skip_row[:, cols] * dyp).astype(BF16)
+        gx[0, :, cols] = (nn(w_t[pair], stack) + skip_row[:, cols] * dyp).astype(BF16)
         for j in range(2):
             h = pair * 2 + j
             t_h = d_w[:, j * TOKENS : (j + 1) * TOKENS] * ed[h]
@@ -328,8 +401,8 @@
             s_h = t_h * table
             row_sums = jnp.where(lane == h, jnp.sum(s_h, axis=1, keepdims=True), row_sums)
             col_sums = jnp.where(sub == h, jnp.sum(s_h, axis=0, keepdims=True), col_sums)
-    gc[...] = nn(d_table.astype(BF16), b[...]).astype(BF16)
-    gb[...] = nn(d_table.T.astype(BF16), c_in[...]).astype(BF16)
+    gc[0] = nn(d_table.astype(BF16), b[...]).astype(BF16)
+    gb[0] = nn(d_table.T.astype(BF16), c_in[...]).astype(BF16)
     direct = col_sums.T
     row, col = iota((TOKENS, TOKENS), 0), iota((TOKENS, TOKENS), 1)
     upper = jnp.where(col >= row, 1.0, 0.0)
@@ -337,7 +410,7 @@
     size, rate = pads[1], pads[2]
     d_size = direct / size + rate * carried
     d_step = d_size / (1.0 + jnp.exp(-pads[0]))
-    gstep[...] = d_step[:, :HEADS].astype(BF16)
+    gstep[0] = d_step.T[:HEADS].astype(BF16)
     gbias[...] = jnp.sum(d_step, axis=0, keepdims=True)[:, :HEADS]
     gdecay[...] = jnp.sum(size * rate * carried, axis=0, keepdims=True)[:, :HEADS]
 
@@ -349,24 +422,13 @@
             ).wait_recv()
             got = n_recv[k, cc].astype(F32) * held
             start = cc * HALF + k * WIDTH
-            arriving[:, start : start + WIDTH // 2] = got[:8].astype(BF16)
-            arriving[:, start + WIDTH // 2 : start + WIDTH] = got[8:].astype(BF16)
-
-    stores = [
-        pltpu.make_async_copy(src, dst.at[0] if len(dst.shape) == 3 else dst, out_sem.at[i])
-        for i, (src, dst) in enumerate(
-            (
-                (arriving, arriving_out), (gx, gx_out), (gz, gz_out), (gb, gb_out), (gc, gc_out), (gstep, gstep_out),
-                (gbias, gbias_out), (gdecay, gdecay_out), (gskip, gskip_out), (ggain, ggain_out),
-            )
-        )
-    ]
-    for store in stores:
-        store.start()
-    for store in stores:
-        store.wait()
+            arriving[0, :, start : start + WIDTH // 2] = got[:8].astype(BF16)
+            arriving[0, :, start + WIDTH // 2 : start + WIDTH] = got[8:].astype(BF16)
+
+    gather_copy(0).wait_send()
+    pl.when(sends_far == 1)(gather_copy(1).wait_send)
+    pl.when(forwards == 1)(forward_copy().wait_send)
     for i in range(2):
-        gather_copy(i).wait_send()
         for d in (1, 2, 3):
             y_gather(i, d).wait_send()
         for d in range(4):
@@ -374,6 +436,15 @@
     for k in range(PARTS):
         for cc in range(2):
             n_copy(k, cc).wait_send()
+
+
+def store_all(*refs):
+    sem = refs[-1]
+    copies = [pltpu.make_async_copy(refs[i], refs[10 + i], sem.at[i]) for i in range(10)]
+    for copy in copies:
+        copy.start()
+    for copy in copies:
+        copy.wait()
 
 
 def solution(mesh):
@@ -413,7 +484,7 @@
             ((1, TOKENS, CHANNELS), BF16),
             ((1, TOKENS, STATE), BF16),
             ((1, TOKENS, STATE), BF16),
-            ((1, TOKENS, HEADS), BF16),
+            ((1, HEADS, TOKENS), BF16),
             ((1, HEADS), F32),
             ((1, HEADS), F32),
             ((1, HEADS), F32),
@@ -425,28 +496,26 @@
     scratch = [
         vmem((TOKENS, CHANNELS), BF16), vmem((ROWS, D), BF16), vmem((CHANNELS, D), BF16), vmem((1, 16), jnp.int32),
         vmem((TOKENS, CHANNELS), BF16), vmem((TOKENS, CHANNELS), BF16), vmem((TOKENS, STATE), BF16),
-        vmem((TOKENS, STATE), BF16), vmem((TOKENS, HEADS), BF16), vmem((1, HEADS), F32), vmem((1, HEADS), F32),
+        vmem((TOKENS, STATE), BF16), vmem((HEADS, TOKENS), BF16), vmem((1, HEADS), F32), vmem((1, HEADS), F32),
         vmem((1, HEADS), F32), vmem((1, CHANNELS), F32), vmem((ROWS, D), BF16),
         vmem((16, HALF), BF16), vmem((16, 16, HALF), BF16), vmem((TOKENS, D), BF16), vmem((TOKENS, CHANNELS), BF16),
         vmem((TOKENS, WIDTH), F32), vmem((PARTS, TOKENS, WIDTH), BF16), vmem((PARTS, TOKENS, WIDTH), F32),
-        vmem((PARTS, TOKENS, WIDTH), BF16), vmem((PARTS, TOKENS, WIDTH), BF16), vmem((PARTS, 3, 32, WIDTH), BF16),
-        vmem((PARTS, 32, WIDTH), F32), vmem((PARTS, 16, WIDTH), BF16), vmem((PARTS, 16, WIDTH), BF16),
+        vmem((PARTS, TOKENS, WIDTH), BF16), vmem((PARTS, TOKENS, WIDTH), BF16), vmem((2, PARTS, 3, 16, WIDTH), BF16),
+        vmem((PARTS, 16, WIDTH), F32), vmem((PARTS, 16, WIDTH), BF16), vmem((PARTS, 16, WIDTH), BF16),
         vmem((PARTS, 2, 16, WIDTH // 2), BF16), vmem((PARTS, 2, 16, WIDTH // 2), BF16),
         vmem((3, TOKENS, 128), F32), vmem((HEADS, TOKENS, TOKENS), F32), vmem((HEADS // 2, TOKENS, 2 * TOKENS), BF16),
         vmem((HEADS // 2, 2 * TOKENS, 128), BF16), vmem((TOKENS, TOKENS), F32), vmem((TOKENS, CHANNELS), F32),
         vmem((TOKENS, CHANNELS), F32), vmem((TOKENS, CHANNELS), F32), vmem((TOKENS, CHANNELS), F32),
-        vmem((ROWS, D), BF16), vmem((TOKENS, CHANNELS), BF16), vmem((TOKENS, CHANNELS), BF16),
-        vmem((TOKENS, STATE), BF16), vmem((TOKENS, STATE), BF16), vmem((TOKENS, HEADS), BF16), vmem((1, HEADS), F32),
-        vmem((1, HEADS), F32), vmem((1, HEADS), F32), vmem((1, CHANNELS), F32),
-        dma((13,)), dma((2, PARTS)), dma((10,)), dma((16,)), dma((16,)), dma((PARTS,)), dma((PARTS,)),
-        dma((PARTS, 3)), dma((PARTS, 3)), dma((PARTS,)), dma((PARTS,)), dma((PARTS, 2)), dma((PARTS, 2)),
+        dma((13,)), dma((2, PARTS)), pltpu.SemaphoreType.REGULAR((2,)), dma((17,)), dma((16,)), dma((2, PARTS)), dma((2, PARTS)),
+        dma((2, PARTS, 3)), dma((2, PARTS, 3)), dma((PARTS,)), dma((PARTS,)), dma((PARTS, 2)), dma((PARTS, 2)),
     ]
-    any_space = pl.BlockSpec(memory_space=pl.ANY)
+    in_hbm = pl.BlockSpec(memory_space=pltpu.HBM)
+    in_vmem = pl.BlockSpec(memory_space=pltpu.VMEM)
     call = pl.pallas_call(
         kernel,
-        out_shape=out_shape,
-        in_specs=[any_space] * 14,
-        out_specs=[any_space] * 10,
+        out_shape=[pltpu.VMEM(out.shape, out.dtype) for out in out_shape],
+        in_specs=[in_hbm] * 14,
+        out_specs=[in_vmem] * 10,
         scratch_shapes=scratch,
         compiler_params=pltpu.CompilerParams(
             collective_id=0, has_side_effects=True, vmem_limit_bytes=48 * 1024 * 1024
@@ -454,7 +523,22 @@
         cost_estimate=pl.CostEstimate(flops=1_200_000_000, bytes_accessed=6_000_000, transcendentals=500_000),
     )
 
+    hand_out = pl.pallas_call(
+        store_all,
+        out_shape=out_shape,
+        in_specs=[in_vmem] * 10,
+        out_specs=[in_hbm] * 10,
+        scratch_shapes=[dma((10,))],
+        cost_estimate=pl.CostEstimate(flops=0, bytes_accessed=900_000, transcendentals=0),
+    )
+
     def on_device(*blocks):
-        return tuple(call(*blocks))
+        blocks = list(blocks)
+        blocks[8] = jnp.swapaxes(blocks[8], 1, 2)
+        blocks = [pltpu.with_memory_space_constraint(block, pltpu.HBM) for block in blocks]
+        held = [pltpu.with_memory_space_constraint(result, pltpu.VMEM) for result in call(*blocks)]
+        results = list(hand_out(*held))
+        results[5] = jnp.swapaxes(results[5], 1, 2)
+        return tuple(results)
 
     return jax.shard_map(on_device, mesh=mesh, in_specs=in_specs, out_specs=out_specs, check_vma=False)

time: 64.9 us -> 50.1 us (0.77)
  the two profiles are of different devices: /device:TPU:7 before, /device:TPU:1 now
where the time goes in v2:
time: 50.1 us; the launch traced here: 50 us
  Pallas kernels  49.4 us (99%)
  between operations  0.66 us (1%)
    pallas_call x1, Pallas kernels, on_device(): call(*blocks)  48.5 us

profile of v2, /device:TPU:1, one launch (start us, length us, event | category | flops | bytes accessed | tf_op | source)
XLA Modules:
  0.0 50.0 jit_solution(15806682967673632200)
XLA Ops:
  0.6 48.5 %shard_map.213 = (bf16[1,8,4096]{2,1,0:T(8,128)(2,1)S(1)}, bf16[1,128,512]{2,1,0:T(8,128)(2,1)S(1)}, bf16[1,128,512]{2,1,0:T(8,128)(2,1)S(1)}, bf16[1,128,128]{2...) custom-call(bf16[1,128,512]{2,1,0:T(8,128)(2,1)} %mixed_hbm.1, ...), custom_call_target="tpu_custom_call" | custom-call | flops 1200000000 | bytes 6000000 | tf_op jit(solution)/shard_map/pallas_call | solution.py:539
  49.2 0.8 %shard_map.214 = (bf16[1,8,4096]{2,1,0:T(8,128)(2,1)}, bf16[1,128,512]{2,1,0:T(8,128)(2,1)}, bf16[1,128,512]{2,1,0:T(8,128)(2,1)}, bf16[1,128,128]{2,1,0:T(8,128...) custom-call(bf16[1,8,4096]{2,1,0:T(8,128)(2,1)S(1)} %get-tuple-eleme, ...), custom_call_target="tpu_custom_call" | custom-call | bytes 900000 | tf_op jit(solution)/shard_map/pallas_call | solution.py:540

commit v3 on v2

--- a/solution.py
+++ b/solution.py
@@ -58,9 +58,9 @@
     bias_hbm, decay_hbm, skip_hbm, gain_hbm, up_hbm,
     arriving, gx, gz, gb, gc, gstep, gbias, gdecay, gskip, ggain,
     mixed, resid, weight, exps, x, z, b, c_in, raw, bias, decay, skip, gain, up,
-    up_send, gathered, rows_in, scaled, temp, p_send, p_own, s_recv, q_send, y_recv, r_sum, z_send, z_recv, n_send, n_recv,
+    up_send, gathered, rows_in, scaled, temp, p_send, p_own, s_recv, q_send, y_recv, r_sum, z_send, z_recv, n_send, n_recv, f_send, f_recv,
     pads, ed, w_t, x_stack, g_table, y_val, normed, q_gate, s_gate,
-    load_sem, w_sem, ready, ag_send, ag_recv, sib_send, sib_recv, ys_send, ys_recv, zs_send, zs_recv, ns_send, ns_recv,
+    load_sem, w_sem, ready, ag_send, ag_recv, sib_send, sib_recv, ys_send, ys_recv, zs_send, zs_recv, ns_send, ns_recv, fs_send, fs_recv,
 ):
     p, t = lax.axis_index("pipe"), lax.axis_index("tp")
     n_pipe = lax.axis_size("pipe")
@@ -124,15 +124,20 @@
     sends_far = odd + at_start
     gets_far = (1 - odd) + at_half
     forwards = odd * (1 - from_end)
+    swaps_out = 1 - forwards
+    swaps_in = (1 - odd) + at_half
+    gets_sum = (1 - odd) * (1 - from_half)
     partners = [(device, 1, 0, 1, 0, 0) for device in (sibling, *y_peer[1:])]
     partners += [
         (opposite, 1, first, 1, 1 - first, 1),
         ((after, at(y, near, core)), 1, at_half, 1, from_end, 0),
         ((after, at(y, near, 1 - core)), 1, at_half, 0, 0, 0),
-        ((after, at(y, 1 - near, core)), 0, 0, gets_far, near, 1),
+        ((after, at(y, 1 - near, core)), forwards, first * (1 - near), gets_far, near, 1),
+        ((after, at(y, 1 - near, 1 - core)), forwards, first * (1 - near), 0, 0, 1),
         ((before, at(y, near_down, core)), 1, at_start, 1, from_half, 0),
         ((before, at(y, near_down, 1 - core)), 0, 0, 1, from_half, 0),
-        ((before, at(y, far_down, core)), sends_far, first, 0, 0, 1),
+        ((before, at(y, far_down, core)), sends_far, first, gets_sum, (1 - first) * (1 - far_down), 1),
+        ((before, at(y, far_down, 1 - core)), 0, 0, gets_sum, (1 - first) * (1 - far_down), 1),
     ]
     barrier = pltpu.get_barrier_semaphore()
 
@@ -213,7 +218,7 @@
     def forward_copy():
         return block_copy(0, 0, opposite, ag_send.at[16])
 
-    @pl.when(late)
+    @pl.when((1 - first) * (1 - from_end) == 1)
     def _():
         arrived(slot(0, 0, core))
         pl.when(forwards == 1)(forward_copy().start)
@@ -252,6 +257,11 @@
 
     def z_copy(k):
         return remote(z_send.at[k], z_recv.at[k], zs_send.at[k], zs_recv.at[k], opposite)
+
+    def f_copy(k, cc):
+        return remote(
+            f_send.at[k, cc], f_recv.at[k, core], fs_send.at[k, cc], fs_recv.at[k, core], (after, at(y, 1 - near, cc))
+        )
 
     pair_sum(0)
 
@@ -305,8 +315,12 @@
     mixer_forward()
 
     for k in range(PARTS):
-        z_send[k] = section_sum(0, k).astype(BF16)
-        pl.when(late)(z_copy(k).start)
+        total = section_sum(0, k)
+        z_send[k] = total.astype(BF16)
+        pl.when(late & (swaps_out == 1))(z_copy(k).start)
+        for cc in range(2):
+            f_send[k, cc] = fold(total[cc * ROWS : (cc + 1) * ROWS]).astype(BF16)
+            pl.when(forwards * (1 - first * (1 - near)) == 1)(f_copy(k, cc).start)
     pair_sum(1)
 
     def hand_on(i):
@@ -323,21 +337,23 @@
     def _():
         pl.when(readied[0] > 0)(lambda: pl.semaphore_wait(ready.at[0], readied[0]))
         pl.when(at_start == 1)(gather_copy(0).start)
-        arrived(slot(0, 0, core))
-
+
+    pl.when(first + from_end == 1)(lambda: arrived(slot(0, 0, core)))
     hand_on(0)
 
     @pl.when(z_hi == 0)
     def _():
         pl.semaphore_wait(ready.at[1], readied[1])
         for k in range(PARTS):
-            z_copy(k).start()
+            pl.when(swaps_out == 1)(z_copy(k).start)
+            for cc in range(2):
+                pl.when(forwards * (1 - near) == 1)(f_copy(k, cc).start)
         pl.when(sends_far == 1)(gather_copy(1).start)
         pl.when(forwards == 1)(forward_copy().start)
 
     for k in range(PARTS):
         r_sum[k] = section_sum(1, k)
-    hand_over(0)
+
     def n_copy(k, cc):
         return remote(
             n_send.at[k, cc], n_recv.at[k, core], ns_send.at[k, cc], ns_recv.at[k, core], (after, at(y, near, cc))
@@ -345,17 +361,25 @@
 
     def produce():
         for k in range(PARTS):
-            z_copy(k).wait()
-            total = r_sum[k] + z_recv[k].astype(F32)
+            pl.when(swaps_out == 1)(z_copy(k).wait_send)
+
+            @pl.when(swaps_in == 1)
+            def _(k=k):
+                z_copy(k).wait_recv()
+                r_sum[k] += z_recv[k].astype(F32)
+
+            total = r_sum[k]
             for cc in range(2):
                 n_send[k, cc] = fold(total[cc * ROWS : (cc + 1) * ROWS]).astype(BF16)
                 n_copy(k, cc).start()
 
-    pl.when(late)(produce)
+    pl.when(swaps_in == 0)(produce)
+    hand_over(0)
+    pl.when(late & (swaps_in == 1))(produce)
     arrived(slot(1, 0, core))
     hand_on(1)
     hand_over(1)
-    pl.when(z_hi == 0)(produce)
+    pl.when(first * swaps_in == 1)(produce)
 
     for i in range(2):
         for d in range(4):
@@ -420,10 +444,20 @@
             remote(
                 n_send.at[k, 0], n_recv.at[k, cc], ns_send.at[k, 0], ns_recv.at[k, cc], sibling
             ).wait_recv()
-            got = n_recv[k, cc].astype(F32) * held
-            start = cc * HALF + k * WIDTH
-            arriving[0, :, start : start + WIDTH // 2] = got[:8].astype(BF16)
-            arriving[0, :, start + WIDTH // 2 : start + WIDTH] = got[8:].astype(BF16)
+
+            def keep(got, start=cc * HALF + k * WIDTH):
+                got = got * held
+                arriving[0, :, start : start + WIDTH // 2] = got[:8].astype(BF16)
+                arriving[0, :, start + WIDTH // 2 : start + WIDTH] = got[8:].astype(BF16)
+
+            @pl.when(gets_sum == 1)
+            def _(k=k, cc=cc, keep=keep):
+                remote(
+                    f_send.at[k, 0], f_recv.at[k, cc], fs_send.at[k, 0], fs_recv.at[k, cc], sibling
+                ).wait_recv()
+                keep(n_recv[k, cc].astype(F32) + f_recv[k, cc].astype(F32))
+
+            pl.when(gets_sum == 0)(lambda k=k, cc=cc, keep=keep: keep(n_recv[k, cc].astype(F32)))
 
     gather_copy(0).wait_send()
     pl.when(sends_far == 1)(gather_copy(1).wait_send)
@@ -436,6 +470,7 @@
     for k in range(PARTS):
         for cc in range(2):
             n_copy(k, cc).wait_send()
+            pl.when(forwards == 1)(f_copy(k, cc).wait_send)
 
 
 def store_all(*refs):
@@ -503,11 +538,13 @@
         vmem((PARTS, TOKENS, WIDTH), BF16), vmem((PARTS, TOKENS, WIDTH), BF16), vmem((2, PARTS, 3, 16, WIDTH), BF16),
         vmem((PARTS, 16, WIDTH), F32), vmem((PARTS, 16, WIDTH), BF16), vmem((PARTS, 16, WIDTH), BF16),
         vmem((PARTS, 2, 16, WIDTH // 2), BF16), vmem((PARTS, 2, 16, WIDTH // 2), BF16),
+        vmem((PARTS, 2, 16, WIDTH // 2), BF16), vmem((PARTS, 2, 16, WIDTH // 2), BF16),
         vmem((3, TOKENS, 128), F32), vmem((HEADS, TOKENS, TOKENS), F32), vmem((HEADS // 2, TOKENS, 2 * TOKENS), BF16),
         vmem((HEADS // 2, 2 * TOKENS, 128), BF16), vmem((TOKENS, TOKENS), F32), vmem((TOKENS, CHANNELS), F32),
         vmem((TOKENS, CHANNELS), F32), vmem((TOKENS, CHANNELS), F32), vmem((TOKENS, CHANNELS), F32),
         dma((13,)), dma((2, PARTS)), pltpu.SemaphoreType.REGULAR((2,)), dma((17,)), dma((16,)), dma((2, PARTS)), dma((2, PARTS)),
         dma((2, PARTS, 3)), dma((2, PARTS, 3)), dma((PARTS,)), dma((PARTS,)), dma((PARTS, 2)), dma((PARTS, 2)),
+        dma((PARTS, 2)), dma((PARTS, 2)),
     ]
     in_hbm = pl.BlockSpec(memory_space=pltpu.HBM)
     in_vmem = pl.BlockSpec(memory_space=pltpu.VMEM)

time: 50.1 us -> 38.7 us (0.77)
  the two profiles are of different devices: /device:TPU:1 before, /device:TPU:421 now
where the time goes in v3:
time: 38.7 us; the launch traced here: 38.6 us
  Pallas kernels  37.9 us (98%)
  between operations  0.66 us (2%)
    pallas_call x1, Pallas kernels, on_device(): call(*blocks)  37.1 us
    pallas_call x1, Pallas kernels, on_device(): results = list(hand_out(*held))  0.84 us

profile of v3, /device:TPU:421, one launch (start us, length us, event | category | flops | bytes accessed | tf_op | source)
XLA Modules:
  0.0 38.6 jit_solution(10949490524294107638)
XLA Ops:
  0.6 37.1 %shard_map.213 = (bf16[1,8,4096]{2,1,0:T(8,128)(2,1)S(1)}, bf16[1,128,512]{2,1,0:T(8,128)(2,1)S(1)}, bf16[1,128,512]{2,1,0:T(8,128)(2,1)S(1)}, bf16[1,128,128]{2...) custom-call(bf16[1,128,512]{2,1,0:T(8,128)(2,1)} %mixed_hbm.1, ...), custom_call_target="tpu_custom_call" | custom-call | flops 1200000000 | bytes 6000000 | tf_op jit(solution)/shard_map/pallas_call | solution.py:576
  37.7 0.8 %shard_map.214 = (bf16[1,8,4096]{2,1,0:T(8,128)(2,1)}, bf16[1,128,512]{2,1,0:T(8,128)(2,1)}, bf16[1,128,512]{2,1,0:T(8,128)(2,1)}, bf16[1,128,128]{2,1,0:T(8,128...) custom-call(bf16[1,8,4096]{2,1,0:T(8,128)(2,1)S(1)} %get-tuple-eleme, ...), custom_call_target="tpu_custom_call" | custom-call | bytes 900000 | tf_op jit(solution)/shard_map/pallas_call | solution.py:577

commit v4 on v3

--- a/solution.py
+++ b/solution.py
@@ -103,13 +103,7 @@
         cols = columns(side, k)
         return pltpu.make_async_copy(weight_hbm.at[0, :, cols], weight.at[:, cols], w_sem.at[side, k])
 
-    for name in ("up", "mixed", "exps", "resid"):
-        loads[name].start()
-    for k in range(PARTS):
-        for side in range(2):
-            w_load(side, k).start()
-    for name in ("raw", "bias", "decay", "b", "c", "x", "z", "skip", "gain"):
-        loads[name].start()
+    loads["up"].start()
 
     def flag(condition):
         return jnp.where(condition, 1, 0)
@@ -150,6 +144,14 @@
         pl.when(greet > 0)(lambda device=device: tell(barrier, device))
         greeted += flag(to_it * (1 - to_held) + from_it * from_held > 0)
         readied[which] += to_it * to_held
+
+    for name in ("mixed", "exps", "resid"):
+        loads[name].start()
+    for k in range(PARTS):
+        for side in range(2):
+            w_load(side, k).start()
+    for name in ("raw", "bias", "decay", "b", "c", "x", "z", "skip", "gain"):
+        loads[name].start()
 
     def remote(src, dst, send, recv, device):
         return pltpu.make_async_remote_copy(
@@ -344,50 +346,52 @@
     @pl.when(z_hi == 0)
     def _():
         pl.semaphore_wait(ready.at[1], readied[1])
+        pl.when(sends_far == 1)(gather_copy(1).start)
+        pl.when(forwards == 1)(forward_copy().start)
+
+    for k in range(PARTS):
+        r_sum[k] = section_sum(1, k)
+
+    def n_copy(k, cc):
+        return remote(
+            n_send.at[k, cc], n_recv.at[k, core], ns_send.at[k, cc], ns_recv.at[k, core], (after, at(y, near, cc))
+        )
+
+    def produce():
+        for k in range(PARTS):
+            pl.when(swaps_out == 1)(z_copy(k).wait_send)
+
+            @pl.when(swaps_in == 1)
+            def _(k=k):
+                z_copy(k).wait_recv()
+                r_sum[k] += z_recv[k].astype(F32)
+
+            total = r_sum[k]
+            for cc in range(2):
+                n_send[k, cc] = fold(total[cc * ROWS : (cc + 1) * ROWS]).astype(BF16)
+                n_copy(k, cc).start()
+
+    pl.when(swaps_in == 0)(produce)
+    hand_over(0)
+    @pl.when(z_hi == 0)
+    def _():
         for k in range(PARTS):
             pl.when(swaps_out == 1)(z_copy(k).start)
             for cc in range(2):
                 pl.when(forwards * (1 - near) == 1)(f_copy(k, cc).start)
-        pl.when(sends_far == 1)(gather_copy(1).start)
-        pl.when(forwards == 1)(forward_copy().start)
-
-    for k in range(PARTS):
-        r_sum[k] = section_sum(1, k)
-
-    def n_copy(k, cc):
-        return remote(
-            n_send.at[k, cc], n_recv.at[k, core], ns_send.at[k, cc], ns_recv.at[k, core], (after, at(y, near, cc))
-        )
-
-    def produce():
-        for k in range(PARTS):
-            pl.when(swaps_out == 1)(z_copy(k).wait_send)
-
-            @pl.when(swaps_in == 1)
-            def _(k=k):
-                z_copy(k).wait_recv()
-                r_sum[k] += z_recv[k].astype(F32)
-
-            total = r_sum[k]
-            for cc in range(2):
-                n_send[k, cc] = fold(total[cc * ROWS : (cc + 1) * ROWS]).astype(BF16)
-                n_copy(k, cc).start()
-
-    pl.when(swaps_in == 0)(produce)
-    hand_over(0)
-    pl.when(late & (swaps_in == 1))(produce)
+
     arrived(slot(1, 0, core))
     hand_on(1)
     hand_over(1)
-    pl.when(first * swaps_in == 1)(produce)
+    pl.when(swaps_in == 1)(produce)
 
     for i in range(2):
         for d in range(4):
             arrived(slot(i, d, 1 - core))
     for m in range(8):
-        first, second = gathered[2 * m].astype(F32), gathered[2 * m + 1].astype(F32)
+        lower, upper = gathered[2 * m].astype(F32), gathered[2 * m + 1].astype(F32)
         for j in range(2):
-            part = jnp.concatenate([first[j * 8 : j * 8 + 8], second[j * 8 : j * 8 + 8]], axis=0)
+            part = jnp.concatenate([lower[j * 8 : j * 8 + 8], upper[j * 8 : j * 8 + 8]], axis=0)
             rows_in[m * 16 : m * 16 + 16, j * HALF : (j + 1) * HALF] = part.astype(BF16)
     fed = jnp.where(p == n_pipe - 1, 0.0, 1.0)
     cotangent = nt(rows_in[...], weight[...]) * (scale * fed)

time: 38.7 us -> 38.5 us (level)
  the two profiles are of different devices: /device:TPU:421 before, /device:TPU:325 now
where the time goes in v4:
time: 38.5 us; the launch traced here: 38.4 us
  Pallas kernels  37.7 us (98%)
  between operations  0.66 us (2%)
    pallas_call x1, Pallas kernels, on_device(): call(*blocks)  36.9 us
    pallas_call x1, Pallas kernels, on_device(): results = list(hand_out(*held))  0.84 us

profile of v4, /device:TPU:325, one launch (start us, length us, event | category | flops | bytes accessed | tf_op | source)
XLA Modules:
  0.0 38.4 jit_solution(1712480332121093026)
XLA Ops:
  0.6 36.9 %shard_map.213 = (bf16[1,8,4096]{2,1,0:T(8,128)(2,1)S(1)}, bf16[1,128,512]{2,1,0:T(8,128)(2,1)S(1)}, bf16[1,128,512]{2,1,0:T(8,128)(2,1)S(1)}, bf16[1,128,128]{2...) custom-call(bf16[1,128,512]{2,1,0:T(8,128)(2,1)} %mixed_hbm.1, ...), custom_call_target="tpu_custom_call" | custom-call | flops 1200000000 | bytes 6000000 | tf_op jit(solution)/shard_map/pallas_call | solution.py:580
  37.5 0.8 %shard_map.214 = (bf16[1,8,4096]{2,1,0:T(8,128)(2,1)}, bf16[1,128,512]{2,1,0:T(8,128)(2,1)}, bf16[1,128,512]{2,1,0:T(8,128)(2,1)}, bf16[1,128,128]{2,1,0:T(8,128...) custom-call(bf16[1,8,4096]{2,1,0:T(8,128)(2,1)S(1)} %get-tuple-eleme, ...), custom_call_target="tpu_custom_call" | custom-call | bytes 900000 | tf_op jit(solution)/shard_map/pallas_call | solution.py:581
